TPU v7x, 32 devices: a whole 2x2x4 slice. The times are simulated.
32 devices in a mesh: dp: 8 (over y, x, core), tensor: 4 (over z).
Axes of the slice: x: 2, y: 2, z: 4, core: 2. Of those that a mesh axis runs over, the one named last changes fastest.
Arguments:
- latents: bfloat16 [16, 256, 768], P('dp'), may hold values from -6 to 6
- conditioning: bfloat16 [16, 768], P('dp'), may hold values from -6 to 6
- live_counts: int32 [8], P('dp'), may hold values from 1 to 2, as said below
- ada_weight: bfloat16 [768, 4608], P(None, 'tensor'), may hold values from -0.21875 to 0.21875
- ada_bias: float32 [4608], P('tensor'), may hold values from -3 to 3
- qkv_weight: bfloat16 [768, 3, 768], P(None, None, 'tensor'), may hold values from -4 to 4
- qv_bias: float32 [2, 768], P(None, 'tensor'), may hold values from -3 to 3
- proj_weight: bfloat16 [768, 768], P('tensor'), may hold values from -0.875 to 0.875
- proj_bias: float32 [768], replicated, may hold values from -3 to 3
- dense1_weight: bfloat16 [768, 3072], P(None, 'tensor'), may hold values from -0.21875 to 0.21875
- dense1_bias: float32 [3072], P('tensor'), may hold values from -3 to 3
- dense2_weight: bfloat16 [3072, 768], P('tensor'), may hold values from -0.109375 to 0.109375
- dense2_bias: float32 [768], replicated, may hold values from -3 to 3
- cotangent: bfloat16 [16, 256, 768], P('dp'), may hold values from -6 to 6
Outputs:
- block_output: bfloat16 [16, 256, 768], P('dp')
- grad_latents: float32 [16, 256, 768], P('dp')
- grad_conditioning: float32 [16, 768], P('dp')
- grad_ada_weight: float32 [768, 4608], P('dp', 'tensor')
- grad_ada_bias: float32 [4608], P('tensor')
- grad_qkv_weight: float32 [768, 3, 768], P('dp', None, 'tensor')
- grad_qv_bias: float32 [2, 768], P(None, 'tensor')
- grad_proj_weight: float32 [768, 768], P('tensor', 'dp')
- grad_proj_bias: float32 [768], replicated
- grad_fc1_weight: float32 [768, 3072], P('dp', 'tensor')
- grad_fc1_bias: float32 [3072], P('tensor')
- grad_fc2_weight: float32 [3072, 768], P('tensor', 'dp')
- grad_fc2_bias: float32 [768], replicated
Inputs may be any that keep to these rules, and one draw needn't show every extreme that they name: `live_counts`: each entry counts the live latents of one dp index; they fill its first slots. Some index holds 2, some holds 1.
All inputs are finite; a program needn't handle non-finite values.
Results may differ from a plain program's by a relative error of at most 0.012.
The roundings to bfloat16 on the way count: a program that leaves them out, or rounds other values in their place, can miss the bound.
Values may be sent and summed in bfloat16 or wider, within the bound.
A program may use at most 128 MiB of HBM per device.

v0:
```python
import math

import jax
import jax.numpy as jnp
from jax import lax
from jax.sharding import PartitionSpec as P

HD = 64


EPS = 1e-06
GELU_C = math.sqrt(2.0 / math.pi)


def to_half(values):
    return values.astype(jnp.bfloat16)


def silu_slope(values):
    sig = jax.nn.sigmoid(values)
    return sig * (1.0 + values * (1.0 - sig))


def gelu_slope(values):
    tangent = jnp.tanh(GELU_C * (values + 0.044715 * values * values * values))
    return 0.5 * (1.0 + tangent) + 0.5 * values * (1.0 - tangent * tangent) * GELU_C * (
        1.0 + 3.0 * 0.044715 * values * values
    )


def norm_rows(values):
    center = values - jnp.mean(values, axis=-1, keepdims=True)
    recip = lax.rsqrt(jnp.mean(center * center, axis=-1, keepdims=True) + EPS)
    return (center * recip, recip)


def norm_back(grad_norm, normed, recip):
    return recip * (
        grad_norm
        - jnp.mean(grad_norm, axis=-1, keepdims=True)
        - normed * jnp.mean(grad_norm * normed, axis=-1, keepdims=True)
    )


def contract_lowprec(form, left, right):
    return jnp.einsum(form, left, right, preferred_element_type=jnp.float32)


def place_columns(piece, total_cols, start):
    empty = jnp.zeros(piece.shape[:-1] + (total_cols,), jnp.float32)
    return lax.dynamic_update_slice_in_dim(empty, piece, start, piece.ndim - 1)


def per_device(
    latents,
    conditioning,
    live_counts,
    ada_weight,
    ada_bias,
    qkv_weight,
    qv_bias,
    proj_weight,
    proj_bias,
    dense1_weight,
    dense1_bias,
    dense2_weight,
    dense2_bias,
    cotangent,
):
    lat_cap, seq_len, width = latents.shape
    head_count = qkv_weight.shape[2] // HD
    local_width = head_count * HD
    local_cols = ada_weight.shape[1]
    local_hidden = dense1_weight.shape[1]
    tensor_count = lax.axis_size("tensor")
    tensor_index = lax.axis_index("tensor")
    rows_dev = seq_len // tensor_count
    row_start = tensor_index * rows_dev
    scale_qk = HD ** (-0.5)
    live_mask = (jnp.arange(lat_cap) < live_counts[0]).astype(jnp.float32)[:, None, None]
    cond_f = conditioning.astype(jnp.float32)
    silu_b = to_half(jax.nn.silu(cond_f))
    mod_part = jnp.dot(silu_b, ada_weight, preferred_element_type=jnp.float32) + ada_bias
    modulation = lax.all_gather(mod_part, "tensor", axis=1, tiled=True)
    blocks = modulation.reshape(lat_cap, 6, width)[:, :, None, :]
    shift_one, scale_one, gate_one = (blocks[:, 0], blocks[:, 1], blocks[:, 2])
    shift_two, scale_two, gate_two = (blocks[:, 3], blocks[:, 4], blocks[:, 5])
    tokens_f = latents.astype(jnp.float32)
    norm_one, recip_one = norm_rows(tokens_f)
    h_one = to_half(norm_one * (1.0 + scale_one) + shift_one)
    qkv_rows = contract_lowprec("lsd,dce->lsce", h_one, qkv_weight)
    queries = to_half(qkv_rows[:, :, 0] + qv_bias[0]).reshape(lat_cap, seq_len, head_count, HD)
    key_rows = to_half(qkv_rows[:, :, 1]).reshape(lat_cap, seq_len, head_count, HD)
    value_rows = to_half(qkv_rows[:, :, 2] + qv_bias[1]).reshape(lat_cap, seq_len, head_count, HD)
    scores = contract_lowprec("lqhe,lkhe->lhqk", queries, key_rows) * scale_qk
    log_total = jax.nn.logsumexp(scores, axis=-1, keepdims=True)
    probs_b = to_half(jnp.exp(scores - log_total))
    attended = to_half(contract_lowprec("lhqk,lkhe->lqhe", probs_b, value_rows)).reshape(
        lat_cap, seq_len, local_width
    )
    attn_part = contract_lowprec("lsd,de->lse", attended, proj_weight)
    attn_branch = lax.psum_scatter(attn_part, "tensor", scatter_dimension=1, tiled=True) + proj_bias
    tokens_own = lax.dynamic_slice_in_dim(tokens_f, row_start, rows_dev, 1)
    x_one = tokens_own + gate_one * attn_branch
    norm_two, recip_two = norm_rows(x_one)
    hidden_own = to_half(norm_two * (1.0 + scale_two) + shift_two)
    hidden_second = lax.all_gather(hidden_own, "tensor", axis=1, tiled=True)
    preactivation_rows = contract_lowprec("kow,wz->koz", hidden_second, dense1_weight) + dense1_bias
    activation_lowprec = to_half(jax.nn.gelu(preactivation_rows, approximate=True))
    perceptron_piece = contract_lowprec("jqv,vg->jqg", activation_lowprec, dense2_weight)
    perceptron_branch = (
        lax.psum_scatter(perceptron_piece, "tensor", scatter_dimension=1, tiled=True) + dense2_bias
    )
    output_own = to_half(live_mask * (x_one + gate_two * perceptron_branch))
    cot_own = lax.dynamic_slice_in_dim(cotangent, row_start, rows_dev, 1)
    grad_out = live_mask * cot_own.astype(jnp.float32)
    dgate_two = jnp.sum(grad_out * perceptron_branch, axis=1)
    dmlp = gate_two * grad_out
    dmlp_own_b = to_half(dmlp)
    block_output, perceptron_gradient_lowprec = (
        lax.all_gather(output_own, "tensor", axis=1, tiled=True),
        lax.all_gather(dmlp_own_b, "tensor", axis=1, tiled=True),
    )
    dense2_gradient = contract_lowprec(
        "kby,kbi->yi", activation_lowprec, perceptron_gradient_lowprec
    )
    grad_fc2_part = jnp.sum(dmlp, axis=(0, 1))
    activation_gradient = contract_lowprec(
        "vug,bg->vub", perceptron_gradient_lowprec, dense2_weight
    )
    dpre = activation_gradient * gelu_slope(preactivation_rows)
    preactivation_gradient_lowprec = to_half(dpre)
    dense1_gradient = contract_lowprec("qmw,qmx->wx", hidden_second, preactivation_gradient_lowprec)
    grad_fc1_b = jnp.sum(dpre, axis=(0, 1))
    hidden_gradient_piece = contract_lowprec(
        "hnb,jb->hnj", preactivation_gradient_lowprec, dense1_weight
    )
    hidden_second_gradient = lax.psum_scatter(
        hidden_gradient_piece, "tensor", scatter_dimension=1, tiled=True
    )
    dscale_two = jnp.sum(hidden_second_gradient * norm_two, axis=1)
    dshift_two = jnp.sum(hidden_second_gradient, axis=1)
    dx_one = grad_out + norm_back(hidden_second_gradient * (1.0 + scale_two), norm_two, recip_two)
    dattn = gate_one * dx_one
    dgate_one = jnp.sum(dx_one * attn_branch, axis=1)
    dattn_own_b = to_half(dattn)
    grad_proj_part = jnp.sum(dattn, axis=(0, 1))
    dattn_b = lax.all_gather(dattn_own_b, "tensor", axis=1, tiled=True)
    grad_proj = contract_lowprec("lsd,lse->de", attended, dattn_b)
    dattended = to_half(contract_lowprec("lse,de->lsd", dattn_b, proj_weight)).reshape(
        lat_cap, seq_len, head_count, HD
    )
    scores_again = contract_lowprec("lqhe,lkhe->lhqk", queries, key_rows) * scale_qk
    probs = jnp.exp(scores_again - log_total)
    probs_again = to_half(probs)
    dprobs = contract_lowprec("lqhe,lkhe->lhqk", dattended, value_rows)
    delta = jnp.sum(probs * dprobs, axis=-1, keepdims=True)
    dscores_b = to_half(probs * (dprobs - delta) * scale_qk)
    dquery = contract_lowprec("lhqk,lkhe->lqhe", dscores_b, key_rows).reshape(
        lat_cap, seq_len, local_width
    )
    dkey = contract_lowprec("lhqk,lqhe->lkhe", dscores_b, queries).reshape(
        lat_cap, seq_len, local_width
    )
    dvalue = contract_lowprec("lhqk,lqhe->lkhe", probs_again, dattended).reshape(
        lat_cap, seq_len, local_width
    )
    grad_qv = jnp.stack([jnp.sum(dquery, axis=(0, 1)), jnp.sum(dvalue, axis=(0, 1))], axis=0)
    dqkv_b = to_half(jnp.stack([dquery, dkey, dvalue], axis=2))
    grad_qkv = contract_lowprec("lsd,lsce->dce", h_one, dqkv_b)
    dh_part_one = contract_lowprec("lsce,dce->lsd", dqkv_b, qkv_weight)
    dh_one = lax.psum_scatter(dh_part_one, "tensor", scatter_dimension=1, tiled=True)
    norm_one_own = lax.dynamic_slice_in_dim(norm_one, row_start, rows_dev, 1)
    recip_one_own = lax.dynamic_slice_in_dim(recip_one, row_start, rows_dev, 1)
    dscale_one = jnp.sum(dh_one * norm_one_own, axis=1)
    dshift_one = jnp.sum(dh_one, axis=1)
    grad_own = dx_one + norm_back(dh_one * (1.0 + scale_one), norm_one_own, recip_one_own)
    stats_own = jnp.stack(
        [dshift_one, dscale_one, dgate_one, dshift_two, dscale_two, dgate_two], axis=1
    ).reshape(lat_cap, 1, 6 * width)
    grad_latents, stats_all = (
        lax.all_gather(grad_own, "tensor", axis=1, tiled=True),
        lax.all_gather(stats_own, "tensor", axis=1, tiled=True),
    )
    dmod = jnp.sum(stats_all, axis=1)
    col_start = tensor_index * local_cols
    dmod_local = lax.dynamic_slice_in_dim(dmod, col_start, local_cols, 1)
    dmod_local_b = to_half(dmod_local)
    grad_ada = contract_lowprec("ld,le->de", silu_b, dmod_local_b)
    grad_ada_b = jnp.sum(dmod_local, axis=0)
    cond_part = contract_lowprec("le,de->ld", dmod_local_b, ada_weight)
    grad_conditioning = lax.psum(cond_part, "tensor") * silu_slope(cond_f)
    ada_full = place_columns(grad_ada_b, local_cols * tensor_count, col_start)
    qv_full = place_columns(grad_qv, local_width * tensor_count, tensor_index * local_width)
    fc1_full = place_columns(grad_fc1_b, local_hidden * tensor_count, tensor_index * local_hidden)
    ada_tot, qv_tot, proj_tot, fc1_tot, fc2_tot = lax.psum(
        (ada_full, qv_full, grad_proj_part, fc1_full, grad_fc2_part), ("dp", "tensor")
    )
    bias_ada = lax.dynamic_slice_in_dim(ada_tot, col_start, local_cols, 0)
    bias_qv = lax.dynamic_slice_in_dim(qv_tot, tensor_index * local_width, local_width, 1)
    bias_fc1 = lax.dynamic_slice_in_dim(fc1_tot, tensor_index * local_hidden, local_hidden, 0)
    summed_qkv, summed_proj, summed_fc1, summed_fc2, summed_ada = (
        lax.psum_scatter(grad_qkv, "dp", scatter_dimension=0, tiled=True),
        lax.psum_scatter(grad_proj, "dp", scatter_dimension=1, tiled=True),
        lax.psum_scatter(dense1_gradient, "dp", scatter_dimension=0, tiled=True),
        lax.psum_scatter(dense2_gradient, "dp", scatter_dimension=1, tiled=True),
        lax.psum_scatter(grad_ada, "dp", scatter_dimension=0, tiled=True),
    )
    return (
        block_output,
        grad_latents,
        grad_conditioning,
        summed_ada,
        bias_ada,
        summed_qkv,
        bias_qv,
        summed_proj,
        proj_tot,
        summed_fc1,
        bias_fc1,
        summed_fc2,
        fc2_tot,
    )


def solution(mesh):
    placed = (
        P("dp", None, None),
        P("dp", None),
        P("dp"),
        P(None, "tensor"),
        P("tensor"),
        P(None, None, "tensor"),
        P(None, "tensor"),
        P("tensor", None),
        P(),
        P(None, "tensor"),
        P("tensor"),
        P("tensor", None),
        P(),
        P("dp", None, None),
    )
    return jax.shard_map(
        per_device,
        mesh=mesh,
        in_specs=placed,
        out_specs=(
            P("dp", None, None),
            P("dp", None, None),
            P("dp", None),
            P("dp", "tensor"),
            P("tensor"),
            P("dp", None, "tensor"),
            P(None, "tensor"),
            P("tensor", "dp"),
            P(),
            P("dp", "tensor"),
            P("tensor"),
            P("tensor", "dp"),
            P(),
        ),
        check_vma=False,
    )
```

profile of v0, /device:TPU:0, one launch (start us, length us, event | category | flops | bytes accessed | tf_op | source)
XLA Modules:
  0.0 543.2 jit_solution(3779687220311500372)
XLA Ops:
  9.7 14.8 %all_gather.21 = f32[2,4608]{1,0:T(2,128)S(1)} all-gather(f32[2,1152]{1,0:T(2,128)S(1)} %convolution_add_fusion), channel_id=1, replica_groups=mesh['dp'=8,'tensor'=4] {'tensor'}, dimensions={1}, use_global_device_ids=true | all-gather | bytes 46080 | tf_op jit(solution)/shard_map/all_gather | solution.py:84
  34.7 2.4 convert_element_type.74
  37.1 34.0 %reduce-scatter.12.cloned.1.call-done = f32[2,64,768]{2,1,0:T(8,128)} async-done(((f32[2,256,768]{2,1,0:T(8,128)}), f32[2,64,768]{2,1,0:T(8,128)}) %reduce-scatter.12.cloned.1.call-update) | async-done | bytes 393232 | tf_op jit(solution)/shard_map/reduce_scatter | solution.py:102
  73.3 18.2 %all_gather.22 = bf16[2,256,768]{2,1,0:T(8,128)(2,1)S(1)} all-gather(bf16[2,64,768]{2,1,0:T(8,128)(2,1)S(1)} %add_convert_fusion.1), channel_id=1, replica_groups=mesh['dp'=8,'tensor'=4] {'tensor'}, dimensions={1}, use_global_device_ids=true | all-gather | bytes 983040 | tf_op jit(solution)/shard_map/all_gather | solution.py:107
  94.3 2.2 fusion.28
  97.9 33.4 %reduce-scatter.14.cloned.1.call-done = f32[2,64,768]{2,1,0:T(8,128)} async-done(((f32[2,256,768]{2,1,0:T(8,128)}), f32[2,64,768]{2,1,0:T(8,128)}) %reduce-scatter.14.cloned.1.call-update) | async-done | bytes 393232 | tf_op jit(solution)/shard_map/reduce_scatter | solution.py:112
  131.3 2.8 fusion.50
  134.0 18.0 %all_gather.24 = bf16[2,256,768]{2,1,0:T(8,128)(2,1)S(1)} all-gather(bf16[2,64,768]{2,1,0:T(8,128)(2,1)S(1)} %get-tuple-element.37), channel_id=1, replica_groups=mesh['dp'=8,'tensor'=4] {'tensor'}, dimensions={1}, use_global_device_ids=true | all-gather | bytes 983040 | tf_op jit(solution)/shard_map/all_gather | solution.py:122
  152.1 3.8 fusion.89
  156.7 2.0 fusion.30
  158.8 34.8 %reduce-scatter.16.cloned.1.call-done = f32[2,64,768]{2,1,0:T(8,128)} async-done(((f32[2,256,768]{2,1,0:T(8,128)}), f32[2,64,768]{2,1,0:T(8,128)}) %reduce-scatter.16.cloned.1.call-update) | async-done | bytes 393232 | tf_op jit(solution)/shard_map/reduce_scatter | solution.py:138
  193.5 2.0 multiply_reduce_fusion.3
  195.5 2.2 multiply_reduce_fusion.9
  197.7 18.3 %all_gather.25 = bf16[2,256,768]{2,1,0:T(8,128)(2,1)S(1)} all-gather(bf16[2,64,768]{2,1,0:T(8,128)(2,1)S(1)} %multiply_convert_fusion.2), channel_id=1, replica_groups=mesh['dp'=8,'tensor'=4] {'tensor'}, dimensions={1}, use_global_device_ids=true | all-gather | bytes 983040 | tf_op jit(solution)/shard_map/all_gather | solution.py:148
  219.0 3.9 fusion.83
  222.9 3.4 fusion.33
  228.1 2.0 convolution_bitcast_fusion.3
  234.1 30.7 %reduce-scatter.18.cloned.1.call-done = f32[2,64,768]{2,1,0:T(8,128)} async-done(((f32[2,256,768]{2,1,0:T(8,128)}), f32[2,64,768]{2,1,0:T(8,128)}) %reduce-scatter.18.cloned.1.call-update) | async-done | bytes 393232 | tf_op jit(solution)/shard_map/reduce_scatter | solution.py:172
  266.1 2.0 multiply_add_fusion.1
  268.2 3.6 convolution_bitcast_fusion.2
  273.0 3.8 convolution_bitcast_fusion.1
  278.0 2.5 convolution_bitcast_fusion
  281.4 13.8 %all_gather.27 = f32[2,4,4608]{2,0,1:T(2,128)S(1)} all-gather(f32[2,1,4608]{2,0,1:T(2,128)S(1)} %reshape.159), channel_id=1, replica_groups=mesh['dp'=8,'tensor'=4] {'tensor'}, dimensions={1}, use_global_device_ids=true | all-gather | bytes 184320 | tf_op jit(solution)/shard_map/all_gather | solution.py:183
  295.4 2.5 fusion.73
  298.7 17.6 %all_gather.23 = bf16[2,256,768]{2,1,0:T(8,128)(2,1)S(1)} all-gather(bf16[2,64,768]{2,1,0:T(8,128)(2,1)S(1)} %copy-done.18), channel_id=1, replica_groups=mesh['dp'=8,'tensor'=4] {'tensor'}, dimensions={1}, use_global_device_ids=true | all-gather | bytes 983040 | tf_op jit(solution)/shard_map/all_gather | solution.py:121
  317.0 1.6 copy.73
  319.0 40.9 %all-reduce = (f32[4608]{0:T(1024)S(1)}, f32[2,768]{1,0:T(2,128)S(1)}, f32[768]{0:T(1024)}, f32[3072]{0:T(1024)S(1)}, f32[768]{0:T(1024)}) all-reduce(f32[4608]{0:T(1024)S(1)} %dynamic_update_slice.9, f32[2,768]{1,0:T(2,128)S(1)} %dynamic_update_slice.10, ...), channel_id=1, replica_groups=mesh['dp'=8,'tensor'=4] {'dp','tensor'}, use_global_device_ids=true, to_apply=%region_25.26 | all-reduce | flops 10752 | bytes 86016 | tf_op jit(solution)/shard_map/psum | solution.py:196
  361.8 10.6 %psum.42 = f32[2,768]{1,0:T(2,128)S(1)} all-reduce(f32[2,768]{1,0:T(2,128)S(1)} %fusion.74), channel_id=1, replica_groups=mesh['dp'=8,'tensor'=4] {'tensor'}, use_global_device_ids=true, to_apply=%region_22.23 | all-reduce | flops 1536 | bytes 12288 | tf_op jit(solution)/shard_map/psum | solution.py:192
  373.7 14.2 %reduce-scatter.24.cloned.1.call-done = f32[96,768]{1,0:T(8,128)} async-done(((f32[768,768]{1,0:T(8,128)}), f32[96,768]{1,0:T(8,128)}) %reduce-scatter.24.cloned.1.call-update) | async-done | bytes 294928 | tf_op jit(solution)/shard_map/reduce_scatter | solution.py:205
  387.9 46.8 %reduce-scatter.26.cloned.1.call-done = f32[768,96]{0,1:T(8,128)} async-done(((f32[768,768]{0,1:T(8,128)}), f32[768,96]{0,1:T(8,128)}) %reduce-scatter.26.cloned.1.call-update) | async-done | bytes 294928 | tf_op jit(solution)/shard_map/reduce_scatter | solution.py:206
  434.7 46.5 %reduce-scatter.22.cloned.1.call-done = f32[96,3,192]{2,0,1:T(8,128)} async-done(((f32[768,3,192]{2,0,1:T(8,128)}), f32[96,3,192]{2,0,1:T(8,128)}) %reduce-scatter.22.cloned.1.call-update) | async-done | bytes 221200 | tf_op jit(solution)/shard_map/reduce_scatter | solution.py:203
  481.1 52.4 %reduce-scatter.20.cloned.1.call-done = f32[96,1152]{1,0:T(8,128)} async-done(((f32[768,1152]{1,0:T(8,128)}), f32[96,1152]{1,0:T(8,128)}) %reduce-scatter.20.cloned.1.call-update) | async-done | bytes 442384 | tf_op jit(solution)/shard_map/reduce_scatter | solution.py:207
  (210 shorter events, 40.3 us)
Async XLA Ops:
  7.2 18.0 %copy-start.2 = (bf16[2,256,768]{2,1,0:T(8,128)(2,1)S(1)}, bf16[2,256,768]{2,1,0:T(8,128)(2,1)}, u32[]{:S(2)}) copy-start(bf16[2,256,768]{2,1,0:T(8,128)(2,1)} %param.14) | copy-start | bytes 2359300
  7.2 18.6 %copy-start.51 = (bf16[768,3,192]{0,2,1:T(8,128)(2,1)S(1)}, bf16[768,3,192]{0,2,1:T(8,128)(2,1)}, u32[]{:S(2)}) copy-start(bf16[768,3,192]{0,2,1:T(8,128)(2,1)} %param.19) | copy-start | bytes 2654212
  7.2 63.9 %reduce-scatter.12.cloned.1.call-start = ((), (), s32[]{:S(2)}) async-start(), calls=%async_computation.9 | async-start | bytes 1966080 | tf_op jit(solution)/shard_map/reduce_scatter | solution.py:102
  30.9 3.7 copy-start.32
  34.6 36.5 %copy-start.34 = (f32[768]{0:T(1024)S(1)}, f32[768]{0:T(1024)}, u32[]{:S(2)}) copy-start(f32[768]{0:T(1024)} %param.22) | copy-start | bytes 9220
  34.6 96.6 %reduce-scatter.14.cloned.1.call-start = ((), (), s32[]{:S(2)}) async-start(), calls=%async_computation.10 | async-start | bytes 1966080 | tf_op jit(solution)/shard_map/reduce_scatter | solution.py:112
  71.1 21.3 %copy-start.49 = (bf16[768,768]{1,0:T(8,128)(2,1)S(1)}, bf16[768,768]{1,0:T(8,128)(2,1)}, u32[]{:S(2)}) copy-start(bf16[768,768]{1,0:T(8,128)(2,1)} %param.23) | copy-start | bytes 3538948
  71.1 21.3 %copy-start.53 = (f32[768]{0:T(1024)S(1)}, f32[768]{0:T(1024)}, u32[]{:S(2)}) copy-start(f32[768]{0:T(1024)} %param.24) | copy-start | bytes 9220
  96.6 34.7 %copy-start.43 = (f32[768]{0:T(1024)S(1)}, f32[768]{0:T(1024)}, u32[]{:S(2)}) copy-start(f32[768]{0:T(1024)} %param.26) | copy-start | bytes 9220
  96.6 96.9 %reduce-scatter.16.cloned.1.call-start = ((), (), s32[]{:S(2)}) async-start(), calls=%async_computation.11 | async-start | bytes 1966080 | tf_op jit(solution)/shard_map/reduce_scatter | solution.py:138
  131.3 20.8 %copy-start.48 = (bf16[768,768]{1,0:T(8,128)(2,1)S(1)}, bf16[768,768]{1,0:T(8,128)(2,1)}, u32[]{:S(2)}) copy-start(bf16[768,768]{1,0:T(8,128)(2,1)} %param.25) | copy-start | bytes 3538948
  152.1 3.8 copy-start.16
  152.1 4.7 copy-start.50
  158.7 106.1 %reduce-scatter.18.cloned.1.call-start = ((), (), s32[]{:S(2)}) async-start(), calls=%async_computation.12 | async-start | bytes 1966080 | tf_op jit(solution)/shard_map/reduce_scatter | solution.py:172
  195.5 21.4 %copy-start.13 = (bf16[192,768]{1,0:T(8,128)(2,1)S(1)}, bf16[192,768]{1,0:T(8,128)(2,1)}, u32[]{:S(2)}) copy-start(bf16[192,768]{1,0:T(8,128)(2,1)} %param.21) | copy-start | bytes 884740
  197.7 19.6 %copy-start.7 = (f32[2,64,768]{2,1,0:T(8,128)}, f32[2,64,768]{2,1,0:T(8,128)S(1)}, u32[]{:S(2)}) copy-start(f32[2,64,768]{2,1,0:T(8,128)S(1)} %get-tuple-element.32) | copy-start | bytes 1179652
  197.7 19.6 %copy-start.6 = (f32[2,256,1,192]{1,3,2,0:T(8,128)S(1)}, f32[2,256,1,192]{1,3,2,0:T(8,128)}, u32[]{:S(2)}) copy-start(f32[2,256,1,192]{1,3,2,0:T(8,128)} %get-tuple-element.35) | copy-start | bytes 1179652
  197.7 19.6 %copy-start.33 = (f32[3,64]{1,0:T(4,128)S(1)}, f32[3,64]{1,0:T(4,128)}, u32[]{:S(2)}) copy-start(f32[3,64]{1,0:T(4,128)} %copy-done.32) | copy-start | bytes 2308
  230.1 2.5 copy-start.5
  230.1 86.9 %reduce-scatter.28.cloned.1.call-start = ((), (), s32[]{:S(2)}) async-start(), calls=%async_computation.18 | async-start | bytes 884736
  234.0 32.2 %copy-start.8 = (f32[2,64,768]{2,1,0:T(8,128)S(1)}, f32[2,64,768]{2,1,0:T(8,128)}, u32[]{:S(2)}) copy-start(f32[2,64,768]{2,1,0:T(8,128)} %copy-done.7) | copy-start | bytes 1179652
  234.0 139.7 %all-gather.2.cloned.1.call-start = ((), (), s32[]{:S(2)}) async-start(), calls=%async_computation.13 | async-start | bytes 1966080 | tf_op jit(solution)/shard_map/all_gather | solution.py:182
  268.2 119.7 %reduce-scatter.24.cloned.1.call-start = ((), (), s32[]{:S(2)}) async-start(), calls=%async_computation.16 | async-start | bytes 2654208 | tf_op jit(solution)/shard_map/reduce_scatter | solution.py:205
  271.9 162.8 %reduce-scatter.26.cloned.1.call-start = ((), (), s32[]{:S(2)}) async-start(), calls=%async_computation.17 | async-start | bytes 2654208 | tf_op jit(solution)/shard_map/reduce_scatter | solution.py:206
  276.9 204.2 %reduce-scatter.22.cloned.1.call-start = ((), (), s32[]{:S(2)}) async-start(), calls=%async_computation.15 | async-start | bytes 2654208 | tf_op jit(solution)/shard_map/reduce_scatter | solution.py:203
  280.6 14.8 %copy-start.21 = (bf16[2,768]{1,0:T(2,128)(2,1)S(1)}, bf16[2,768]{1,0:T(2,128)(2,1)}, u32[]{:S(2)}) copy-start(bf16[2,768]{1,0:T(2,128)(2,1)} %param.15) | copy-start | bytes 9220
  280.6 253.0 %reduce-scatter.20.cloned.1.call-start = ((), (), s32[]{:S(2)}) async-start(), calls=%async_computation.14 | async-start | bytes 3981312 | tf_op jit(solution)/shard_map/reduce_scatter | solution.py:207
  297.8 18.5 %copy-start.44 = (f32[768]{0:T(1024)S(1)}, f32[768]{0:T(1024)}, u32[]{:S(2)}) copy-start(f32[768]{0:T(1024)} %get-tuple-element.53) | copy-start | bytes 9220
  297.8 18.8 %copy-start.45 = (f32[3,64]{1,0:T(4,128)S(1)}, f32[3,64]{1,0:T(4,128)}, u32[]{:S(2)}) copy-start(f32[3,64]{1,0:T(4,128)} %get-tuple-element.39) | copy-start | bytes 2308
  297.8 18.9 %copy-start.39 = (f32[3,64]{1,0:T(4,128)S(1)}, f32[3,64]{1,0:T(4,128)}, u32[]{:S(2)}) copy-start(f32[3,64]{1,0:T(4,128)} %get-tuple-element.41) | copy-start | bytes 2308
  297.8 21.2 %copy-start.35 = (f32[768]{0:T(1024)S(1)}, f32[768]{0:T(1024)}, u32[]{:S(2)}) copy-start(f32[768]{0:T(1024)} %get-tuple-element.17) | copy-start | bytes 9220
  297.8 21.2 %copy-start.36 = (f32[768]{0:T(1024)S(1)}, f32[768]{0:T(1024)}, u32[]{:S(2)}) copy-start(f32[768]{0:T(1024)} %get-tuple-element.21) | copy-start | bytes 9220
  (38 other events, 49.6 us)
Sparse Core Ops, SparseCore 0:
  34.7 36.3 reduce-scatter.11
  96.7 34.5 reduce-scatter.13
  158.8 34.6 reduce-scatter.15
  230.2 34.5 reduce-scatter.17
  268.4 33.9 reduce-scatter.27
  304.4 37.7 all-gather.1
  346.1 41.6 reduce-scatter.23
  392.2 42.4 reduce-scatter.25
  438.6 42.5 reduce-scatter.21
  485.4 48.0 reduce-scatter.19
where the time goes:
time: 544 us; the launch traced here: 543 us
  waiting for transfers between devices  293 us (54%)
  blocking collectives  152 us (28%)
  matrix products  41.7 us (8%)
  local copies, waits for them, and re-layouts  22.5 us (4%)
  other arithmetic  18 us (3%)
  between operations  15.4 us (3%)
    reduce_scatter x1, waiting for transfers between devices, per_device(): lax.psum_scatter(grad_ada, 'dp', scatter_dimension=0, tiled=True)  52.4 us
    reduce_scatter x1, waiting for transfers between devices, per_device(): lax.psum_scatter(dense2_gradient, 'dp', scatter_dimension=1, tiled=True)  46.8 us
    reduce_scatter x1, waiting for transfers between devices, per_device(): lax.psum_scatter(grad_qkv, 'dp', scatter_dimension=0, tiled=True)  46.5 us
    psum x1, blocking collectives, per_device(): lax.psum((ada_full, qv_full, grad_proj_part, fc1_full, grad_fc2_part), ('...  40.9 us
    dot_general x20, matrix products, contract_lowprec(): return jnp.einsum(form, left, right, preferred_element_type=jnp.float32)  40.7 us
    reduce_scatter x1, waiting for transfers between devices, per_device(): lax.psum_scatter(hidden_gradient_piece, 'tensor', scatter_dimension=1, ti...  34.8 us
    reduce_scatter x1, waiting for transfers between devices, per_device(): lax.psum_scatter(attn_part, 'tensor', scatter_dimension=1, tiled=True)  34 us
    reduce_scatter x1, waiting for transfers between devices, per_device(): lax.psum_scatter(perceptron_piece, 'tensor', scatter_dimension=1, tiled=T...  33.4 us
  transfers between devices with their start and end apart: 10, of which 8 were waited for; matrix products, arithmetic and copies ran while one was open for 5% of the time, Pallas kernels for 0%

commit v1 on v0

v1 whole, which is shorter than its diff:
```python
import functools
import math

import jax
import jax.numpy as jnp
from jax import lax
from jax.experimental import pallas as pl
from jax.experimental.pallas import tpu as pltpu
from jax.sharding import PartitionSpec as P

HD = 64


EPS = 1e-06
GELU_C = math.sqrt(2.0 / math.pi)


def to_half(values):
    return values.astype(jnp.bfloat16)


def silu_slope(values):
    sig = jax.nn.sigmoid(values)
    return sig * (1.0 + values * (1.0 - sig))


def gelu_slope(values):
    tangent = jnp.tanh(GELU_C * (values + 0.044715 * values * values * values))
    return 0.5 * (1.0 + tangent) + 0.5 * values * (1.0 - tangent * tangent) * GELU_C * (
        1.0 + 3.0 * 0.044715 * values * values
    )


def norm_rows(values):
    center = values - jnp.mean(values, axis=-1, keepdims=True)
    recip = lax.rsqrt(jnp.mean(center * center, axis=-1, keepdims=True) + EPS)
    return (center * recip, recip)


def norm_back(grad_norm, normed, recip):
    return recip * (
        grad_norm
        - jnp.mean(grad_norm, axis=-1, keepdims=True)
        - normed * jnp.mean(grad_norm * normed, axis=-1, keepdims=True)
    )


def contract_lowprec(form, left, right):
    return jnp.einsum(form, left, right, preferred_element_type=jnp.float32)


def exchange_body(kinds, sizes, copy_count, *refs):
    count = len(kinds)
    ins, outs = refs[:count], refs[count : 2 * count]
    send_sem, recv_sem, local_sem = refs[2 * count :]
    axes = [axis for axis in ("tensor", "dp") if any(k[0] == axis for k in kinds)]
    me = {axis: lax.axis_index(axis) for axis in axes}
    barrier = pltpu.get_barrier_semaphore()
    peers = 0
    for axis in axes:
        for step in range(1, sizes[axis]):
            pl.semaphore_signal(
                barrier,
                inc=1,
                device_id={axis: lax.rem(me[axis] + step, sizes[axis])},
                device_id_type=pl.DeviceIdType.MESH,
            )
            peers += 1
    pl.semaphore_wait(barrier, peers)
    started = []
    slot = 0
    for step in range(1, max(sizes.values())):
        for (axis, form), src, dst in zip(kinds, ins, outs):
            size = sizes[axis]
            if step >= size:
                continue
            target = lax.rem(me[axis] + step, size)
            if form == "gather_rows":
                rows = src.shape[1]
                source = src
                place = dst.at[:, pl.ds(pl.multiple_of(me[axis] * rows, rows), rows)]
            elif form == "gather":
                source, place = src, dst.at[me[axis]]
            elif form == "scatter_rows":
                rows = src.shape[1] // size
                source = src.at[:, pl.ds(pl.multiple_of(target * rows, rows), rows)]
                place = dst.at[step - 1]
            else:
                source, place = src.at[target], dst.at[step - 1]
            copy = pltpu.make_async_remote_copy(
                src_ref=source,
                dst_ref=place,
                send_sem=send_sem.at[slot],
                recv_sem=recv_sem.at[slot],
                device_id={axis: target},
                device_id_type=pl.DeviceIdType.MESH,
            )
            copy.start()
            started.append(copy)
            slot += 1
    for index, ((axis, form), src, dst) in enumerate(zip(kinds, ins, outs)):
        if form == "gather_rows":
            rows = src.shape[1]
            place = dst.at[:, pl.ds(pl.multiple_of(me[axis] * rows, rows), rows)]
        elif form == "gather":
            place = dst.at[me[axis]]
        else:
            continue
        copy = pltpu.make_async_copy(src, place, local_sem.at[index])
        copy.start()
        started.append(copy)
    for copy in started:
        copy.wait()


def exchange(ident, *items):
    sizes = {"tensor": lax.axis_size("tensor"), "dp": lax.axis_size("dp")}
    kinds = tuple((axis, form) for axis, form, _ in items)
    shapes = []
    for axis, form, array in items:
        size = sizes[axis]
        if form == "gather_rows":
            shape = (array.shape[0], array.shape[1] * size, array.shape[2])
        elif form == "gather":
            shape = (size,) + array.shape
        elif form == "scatter_rows":
            shape = (size - 1, array.shape[0], array.shape[1] // size, array.shape[2])
        else:
            shape = (size - 1,) + array.shape[1:]
        shapes.append(jax.ShapeDtypeStruct(shape, array.dtype))
    copy_count = sum(sizes[axis] - 1 for axis, _ in kinds)
    return pl.pallas_call(
        functools.partial(exchange_body, kinds, sizes, copy_count),
        out_shape=shapes,
        in_specs=[pl.BlockSpec(memory_space=pl.ANY)] * len(items),
        out_specs=[pl.BlockSpec(memory_space=pl.ANY)] * len(items),
        scratch_shapes=[
            pltpu.SemaphoreType.DMA((copy_count,)),
            pltpu.SemaphoreType.DMA((copy_count,)),
            pltpu.SemaphoreType.DMA((len(items),)),
        ],
        compiler_params=pltpu.CompilerParams(collective_id=ident, has_side_effects=True),
    )(*[array for _, _, array in items])


def sum_rows(piece, arrived, start):
    own = lax.dynamic_slice_in_dim(piece, start, arrived.shape[2], 1).astype(jnp.float32)
    return own + jnp.sum(arrived.astype(jnp.float32), axis=0)


def sum_blocks(pieces, arrived, index):
    own = lax.dynamic_index_in_dim(pieces, index, 0, keepdims=False).astype(jnp.float32)
    return own + jnp.sum(arrived.astype(jnp.float32), axis=0)


def per_device(
    latents,
    conditioning,
    live_counts,
    ada_weight,
    ada_bias,
    qkv_weight,
    qv_bias,
    proj_weight,
    proj_bias,
    dense1_weight,
    dense1_bias,
    dense2_weight,
    dense2_bias,
    cotangent,
):
    lat_cap, seq_len, width = latents.shape
    head_count = qkv_weight.shape[2] // HD
    local_width = head_count * HD
    local_cols = ada_weight.shape[1]
    local_hidden = dense1_weight.shape[1]
    tensor_count = lax.axis_size("tensor")
    tensor_index = lax.axis_index("tensor")
    dp_count = lax.axis_size("dp")
    dp_index = lax.axis_index("dp")
    rows_dev = seq_len // tensor_count
    row_start = tensor_index * rows_dev
    scale_qk = HD ** (-0.5)
    live_mask = (jnp.arange(lat_cap) < live_counts[0]).astype(jnp.float32)[:, None, None]
    cond_f = conditioning.astype(jnp.float32)
    silu_b = to_half(jax.nn.silu(cond_f))
    mod_part = jnp.dot(silu_b, ada_weight, preferred_element_type=jnp.float32) + ada_bias
    mod_all, silu_all = exchange(
        1, ("tensor", "gather", mod_part), ("dp", "gather", silu_b.astype(jnp.float32))
    )
    modulation = jnp.swapaxes(mod_all, 0, 1).reshape(lat_cap, 6 * width)
    blocks = modulation.reshape(lat_cap, 6, width)[:, :, None, :]
    shift_one, scale_one, gate_one = (blocks[:, 0], blocks[:, 1], blocks[:, 2])
    shift_two, scale_two, gate_two = (blocks[:, 3], blocks[:, 4], blocks[:, 5])
    tokens_f = latents.astype(jnp.float32)
    norm_one, recip_one = norm_rows(tokens_f)
    h_one = to_half(norm_one * (1.0 + scale_one) + shift_one)
    qkv_rows = contract_lowprec("lsd,dce->lsce", h_one, qkv_weight)
    queries = to_half(qkv_rows[:, :, 0] + qv_bias[0]).reshape(lat_cap, seq_len, head_count, HD)
    key_rows = to_half(qkv_rows[:, :, 1]).reshape(lat_cap, seq_len, head_count, HD)
    value_rows = to_half(qkv_rows[:, :, 2] + qv_bias[1]).reshape(lat_cap, seq_len, head_count, HD)
    scores = contract_lowprec("lqhe,lkhe->lhqk", queries, key_rows) * scale_qk
    log_total = jax.nn.logsumexp(scores, axis=-1, keepdims=True)
    probs_b = to_half(jnp.exp(scores - log_total))
    attended = to_half(contract_lowprec("lhqk,lkhe->lqhe", probs_b, value_rows)).reshape(
        lat_cap, seq_len, local_width
    )
    attn_part = to_half(contract_lowprec("lsd,de->lse", attended, proj_weight))
    (attn_arrived,) = exchange(2, ("tensor", "scatter_rows", attn_part))
    attn_branch = sum_rows(attn_part, attn_arrived, row_start) + proj_bias
    tokens_own = lax.dynamic_slice_in_dim(tokens_f, row_start, rows_dev, 1)
    x_one = tokens_own + gate_one * attn_branch
    norm_two, recip_two = norm_rows(x_one)
    hidden_own = to_half(norm_two * (1.0 + scale_two) + shift_two)
    (hidden_second,) = exchange(3, ("tensor", "gather_rows", hidden_own))
    preactivation_rows = contract_lowprec("kow,wz->koz", hidden_second, dense1_weight) + dense1_bias
    activation_lowprec = to_half(jax.nn.gelu(preactivation_rows, approximate=True))
    perceptron_piece = to_half(contract_lowprec("jqv,vg->jqg", activation_lowprec, dense2_weight))
    dmlp = gate_two * (live_mask * cotangent.astype(jnp.float32))
    perceptron_gradient_lowprec = to_half(dmlp)
    grad_fc2_part = jnp.sum(dmlp, axis=(0, 1))
    dense2_gradient = to_half(
        contract_lowprec("kbi,kby->iy", perceptron_gradient_lowprec, activation_lowprec)
    ).reshape(dp_count, width // dp_count, local_hidden)
    activation_gradient = contract_lowprec(
        "vug,bg->vub", perceptron_gradient_lowprec, dense2_weight
    )
    dpre = activation_gradient * gelu_slope(preactivation_rows)
    preactivation_gradient_lowprec = to_half(dpre)
    dense1_gradient = to_half(
        contract_lowprec("qmw,qmx->wx", hidden_second, preactivation_gradient_lowprec)
    ).reshape(dp_count, width // dp_count, local_hidden)
    grad_fc1_b = jnp.sum(dpre, axis=(0, 1))
    hidden_gradient_piece = to_half(
        contract_lowprec("hnb,jb->hnj", preactivation_gradient_lowprec, dense1_weight)
    )
    hidden_arrived, perceptron_arrived, fc1_arrived, fc2_arrived = exchange(
        4,
        ("tensor", "scatter_rows", hidden_gradient_piece),
        ("tensor", "scatter_rows", perceptron_piece),
        ("dp", "scatter", dense1_gradient),
        ("dp", "scatter", dense2_gradient),
    )
    summed_fc1 = sum_blocks(dense1_gradient, fc1_arrived, dp_index)
    summed_fc2 = sum_blocks(dense2_gradient, fc2_arrived, dp_index).T
    hidden_second_gradient = sum_rows(hidden_gradient_piece, hidden_arrived, row_start)
    perceptron_branch = sum_rows(perceptron_piece, perceptron_arrived, row_start) + dense2_bias
    output_own = to_half(live_mask * (x_one + gate_two * perceptron_branch))
    cot_own = lax.dynamic_slice_in_dim(cotangent, row_start, rows_dev, 1)
    grad_out = live_mask * cot_own.astype(jnp.float32)
    dgate_two = jnp.sum(grad_out * perceptron_branch, axis=1)
    dscale_two = jnp.sum(hidden_second_gradient * norm_two, axis=1)
    dshift_two = jnp.sum(hidden_second_gradient, axis=1)
    dx_one = grad_out + norm_back(hidden_second_gradient * (1.0 + scale_two), norm_two, recip_two)
    dattn = gate_one * dx_one
    dgate_one = jnp.sum(dx_one * attn_branch, axis=1)
    dattn_own_b = to_half(dattn)
    grad_proj_part = jnp.sum(dattn, axis=(0, 1))
    dattn_b, block_output = exchange(
        5, ("tensor", "gather_rows", dattn_own_b), ("tensor", "gather_rows", output_own)
    )
    grad_proj = contract_lowprec("lse,lsd->ed", dattn_b, attended)
    dattended = to_half(contract_lowprec("lse,de->lsd", dattn_b, proj_weight)).reshape(
        lat_cap, seq_len, head_count, HD
    )
    scores_again = contract_lowprec("lqhe,lkhe->lhqk", queries, key_rows) * scale_qk
    probs = jnp.exp(scores_again - log_total)
    probs_again = to_half(probs)
    dprobs = contract_lowprec("lqhe,lkhe->lhqk", dattended, value_rows)
    delta = jnp.sum(probs * dprobs, axis=-1, keepdims=True)
    dscores_b = to_half(probs * (dprobs - delta) * scale_qk)
    dquery = contract_lowprec("lhqk,lkhe->lqhe", dscores_b, key_rows).reshape(
        lat_cap, seq_len, local_width
    )
    dkey = contract_lowprec("lhqk,lqhe->lkhe", dscores_b, queries).reshape(
        lat_cap, seq_len, local_width
    )
    dvalue = contract_lowprec("lhqk,lqhe->lkhe", probs_again, dattended).reshape(
        lat_cap, seq_len, local_width
    )
    grad_qv = jnp.stack([jnp.sum(dquery, axis=(0, 1)), jnp.sum(dvalue, axis=(0, 1))], axis=0)
    dqkv_b = to_half(jnp.stack([dquery, dkey, dvalue], axis=2))
    grad_qkv = contract_lowprec("lsd,lsce->dce", h_one, dqkv_b)
    dh_part_one = to_half(contract_lowprec("lsce,dce->lsd", dqkv_b, qkv_weight))
    attn_gradient = jnp.concatenate(
        [to_half(grad_qkv).reshape(width, 3 * local_width), to_half(grad_proj)], axis=1
    ).reshape(dp_count, width // dp_count, 4 * local_width)
    dh_arrived, attn_gradient_arrived = exchange(
        6, ("tensor", "scatter_rows", dh_part_one), ("dp", "scatter", attn_gradient)
    )
    summed_attn = sum_blocks(attn_gradient, attn_gradient_arrived, dp_index)
    summed_qkv = summed_attn[:, : 3 * local_width].reshape(-1, 3, local_width)
    summed_proj = summed_attn[:, 3 * local_width :].T
    dh_one = sum_rows(dh_part_one, dh_arrived, row_start)
    norm_one_own = lax.dynamic_slice_in_dim(norm_one, row_start, rows_dev, 1)
    recip_one_own = lax.dynamic_slice_in_dim(recip_one, row_start, rows_dev, 1)
    dscale_one = jnp.sum(dh_one * norm_one_own, axis=1)
    dshift_one = jnp.sum(dh_one, axis=1)
    grad_own = dx_one + norm_back(dh_one * (1.0 + scale_one), norm_one_own, recip_one_own)
    stats_own = jnp.concatenate(
        [
            jnp.stack(
                [dshift_one, dscale_one, dgate_one, dshift_two, dscale_two, dgate_two], axis=1
            ).reshape(lat_cap * 6, width),
            grad_proj_part[None],
        ],
        axis=0,
    )
    grad_gathered, stats_all = exchange(
        7, ("tensor", "gather_rows", to_half(grad_own)), ("tensor", "gather", stats_own)
    )
    grad_latents = grad_gathered.astype(jnp.float32)
    stats_sum = jnp.sum(stats_all, axis=0)
    dmod = stats_sum[: lat_cap * 6].reshape(lat_cap, 6 * width)
    col_start = tensor_index * local_cols
    dmod_local = lax.dynamic_slice_in_dim(dmod, col_start, local_cols, 1)
    cond_part = contract_lowprec("le,de->ld", to_half(dmod_local), ada_weight)
    parts = [
        dmod_local.reshape(-1),
        grad_qv.reshape(-1),
        grad_fc1_b,
        grad_fc2_part,
        stats_sum[lat_cap * 6],
    ]
    packed_all, cond_all = exchange(
        8, ("dp", "gather", jnp.concatenate(parts)[None]), ("tensor", "gather", cond_part)
    )
    grad_conditioning = jnp.sum(cond_all, axis=0) * silu_slope(cond_f)
    packed_all = packed_all[:, 0]
    dmod_cols = lat_cap * local_cols
    dmod_all = packed_all[:, :dmod_cols].reshape(dp_count * lat_cap, local_cols)
    bias_ada = jnp.sum(dmod_all, axis=0)
    block = width // dp_count
    silu_own = lax.dynamic_slice_in_dim(
        to_half(silu_all).reshape(dp_count * lat_cap, width), dp_index * block, block, 1
    )
    summed_ada = contract_lowprec("ld,le->de", silu_own, to_half(dmod_all))
    totals = jnp.sum(packed_all[:, dmod_cols:], axis=0)
    bias_qv, bias_fc1, fc2_tot, proj_tot = jnp.split(
        totals,
        (2 * local_width, 2 * local_width + local_hidden, 2 * local_width + local_hidden + width),
    )
    bias_qv = bias_qv.reshape(2, local_width)
    return (
        block_output,
        grad_latents,
        grad_conditioning,
        summed_ada,
        bias_ada,
        summed_qkv,
        bias_qv,
        summed_proj,
        proj_tot,
        summed_fc1,
        bias_fc1,
        summed_fc2,
        fc2_tot,
    )


def solution(mesh):
    placed = (
        P("dp", None, None),
        P("dp", None),
        P("dp"),
        P(None, "tensor"),
        P("tensor"),
        P(None, None, "tensor"),
        P(None, "tensor"),
        P("tensor", None),
        P(),
        P(None, "tensor"),
        P("tensor"),
        P("tensor", None),
        P(),
        P("dp", None, None),
    )
    return jax.shard_map(
        per_device,
        mesh=mesh,
        in_specs=placed,
        out_specs=(
            P("dp", None, None),
            P("dp", None, None),
            P("dp", None),
            P("dp", "tensor"),
            P("tensor"),
            P("dp", None, "tensor"),
            P(None, "tensor"),
            P("tensor", "dp"),
            P(),
            P("dp", "tensor"),
            P("tensor"),
            P("tensor", "dp"),
            P(),
        ),
        check_vma=False,
    )
```

time: 544 us -> 272 us (0.50)
  waiting for transfers between devices: 293 us -> 0 us
  Pallas kernels: 0 us -> 174 us
  blocking collectives: 152 us -> 0 us
  other arithmetic: 18 us -> 36 us
  between operations: 15.4 us -> 2.28 us
    reduce_scatter x8 -> x0, waiting for transfers between devices: 293 us -> none  [the longest x1 52.4 us: per_device(): lax.psum_scatter(grad_ada, 'dp', scatter_dimension=0, tiled=True)]
    pallas_call x0 -> x8, Pallas kernels: none -> 174 us  [exchange(): pl.pallas_call(functools.partial(exchange_body, kinds, sizes, copy_count)...]
    all_gather x6 -> x0, blocking collectives: 101 us -> none  [the longest x1 18.3 us: per_device(): dattn_b = lax.all_gather(dattn_own_b, 'tensor', axis=1, tiled=True)]
    psum x2 -> x0, blocking collectives: 51.5 us -> none  [the longest x1 40.9 us: per_device(): lax.psum((ada_full, qv_full, grad_proj_part, fc1_full, grad_fc2_part), ('...]
    reduce_sum x3 -> x10, other arithmetic: 2.29 us -> 14.5 us  [the longest x3 4.46 us: sum_rows(): return own + jnp.sum(arrived.astype(jnp.float32), axis=0)]
    unnamed x127 -> x138, local copies, waits for them, and re-layouts: 16.9 us -> 9.68 us
  transfers between devices with their start and end apart: 10 -> 0, of which waited for: 8 -> 0; matrix products, arithmetic and copies ran while one was open for 5% -> 0% of each run, Pallas kernels for 0% -> 0%
where the time goes in v1:
time: 272 us
  Pallas kernels  174 us (64%)
  matrix products  38.4 us (14%)
  other arithmetic  36 us (13%)
  local copies, waits for them, and re-layouts  20.9 us (8%)
    pallas_call x8, Pallas kernels, exchange(): pl.pallas_call(functools.partial(exchange_body, kinds, sizes, copy_count)...  174 us
    dot_general x20, matrix products, contract_lowprec(): return jnp.einsum(form, left, right, preferred_element_type=jnp.float32)  36.7 us
    unnamed x138, local copies, waits for them, and re-layouts  9.68 us

profile of v1, /device:TPU:0, one launch (start us, length us, event | category | flops | bytes accessed | tf_op | source)
XLA Modules:
  0.0 271.5 jit_solution(12143304181564661006)
XLA Ops:
  2.1 1.7 convolution_add_fusion.refs_0_
  4.4 9.7 %shard_map.237 = (f32[4,2,1152]{2,1,0:T(2,128)}, f32[8,2,768]{2,1,0:T(2,128)}) custom-call(f32[2,1152]{1,0:T(2,128)} %convolution_add_fusion.refs_0_, f32[2,768]{1,0:T(2,128)} %fusion.82.refs_1_), custom_call_target="tpu_custom_call" | custom-call | tf_op jit(solution)/shard_map/pallas_call | solution.py:132
  19.2 1.5 fusion.92
  25.7 17.5 %shard_map.238 = bf16[3,2,64,768]{3,2,1,0:T(8,128)(2,1)} custom-call(bf16[2,256,768]{2,1,0:T(8,128)(2,1)} %convolution_convert_fusion.2.refs_0_), custom_call_target="tpu_custom_call" | custom-call | tf_op jit(solution)/shard_map/pallas_call | solution.py:132
  43.2 1.9 convert_reduce_fusion.6
  49.2 19.4 %shard_map.239 = bf16[2,256,768]{2,1,0:T(8,128)(2,1)} custom-call(bf16[2,64,768]{2,1,0:T(8,128)(2,1)} %add_convert_fusion.2.refs_0_), custom_call_target="tpu_custom_call" | custom-call | tf_op jit(solution)/shard_map/pallas_call | solution.py:132
  68.6 2.4 convolution_add_fusion.1
  71.7 2.1 fusion.95
  73.9 1.8 bitcast_convert_fusion.1
  75.7 1.7 convolution_convert_fusion.1.refs_0_
  77.4 2.1 bitcast_convert_fusion
  79.5 1.9 convolution_convert_fusion.refs_1_
  81.5 33.2 %shard_map.240 = (bf16[3,2,64,768]{3,2,1,0:T(8,128)(2,1)}, bf16[3,2,64,768]{3,2,1,0:T(8,128)(2,1)}, bf16[7,96,768]{2,1,0:T(8,128)(2,1)}, bf16[7,96,768]{2,1,0:T(8,128)(2,1)}) custom-call(bf16[2,256,768]{2,1,0:T(8,128)(2,1)} %convolution_convert_fusion.1.refs_0_, bf16[2,256,768]{2,1,0:T(8,128)(2,1)} %convolution_convert_fusion.refs_1_, ...), custom_call_target="tpu_custom_call" | custom-call | tf_op jit(solution)/shard_map/pallas_call | solution.py:132
  114.7 2.7 convert_reduce_fusion
  117.4 1.8 fusion.50
  119.2 1.7 convert_add_fusion.3
  122.3 1.8 multiply_reduce_fusion.3
  124.1 2.8 %multiply_reduce_fusion.2 = (f32[2,768]{1,0:T(2,128)}, bf16[2,64,768]{2,1,0:T(8,128)(2,1)}, f32[768]{0:T(1024)}, f32[2,768]{1,0:T(2,128)}, f32[2,64,768]{2,1,0:T(8,128)S(1)}) fusion(f32[2,64,768]{2,1,0:T(8,128)S(1)} %get-tuple-element.112, f32[768]{0:T(1024)S(1)} %copy-done.50, f32[2]{0:T(128)S(1)} %compare_convert_fusion, ...), kind=kLoop, calls=%fused_computation.74 | loop fusion | flops 2552064 | bytes 2794508 | tf_op jit(solution)/shard_map/reduce_sum | solution.py:251
  128.4 33.6 %shard_map.241 = (bf16[2,256,768]{2,1,0:T(8,128)(2,1)}, bf16[2,256,768]{2,1,0:T(8,128)(2,1)}) custom-call(bf16[2,64,768]{2,1,0:T(8,128)(2,1)} %multiply_convert_fusion.2.refs_0_, bf16[2,64,768]{2,1,0:T(8,128)(2,1)} %get-tuple-element.85.refs_1_), custom_call_target="tpu_custom_call" | custom-call | tf_op jit(solution)/shard_map/pallas_call | solution.py:132
  162.0 1.6 convolution_convert_fusion.3
  163.6 2.8 %fusion.60 = f32[2,3,256,256]{2,3,1,0:T(8,128)} fusion(bf16[2,256,3,64]{1,3,2,0:T(8,128)(2,1)S(1)} %bitcast.128, f32[2,256,3,64]{1,3,2,0:T(8,128)} %bitcast.123, f32[3,64]{1,0:T(4,128)S(1)} %copy-done.40), kind=kOutput, calls=%fused_computation.110 | convolution fusion | flops 50528256 | bytes 2163456 | tf_op jit(solution)/shard_map/lqhe,lkhe->lhqk/dot_general | solution.py:49
  166.4 3.9 %fusion.89 = (f32[3,64]{1,0:T(4,128)}, bf16[2,256,3,64]{1,3,2,0:T(8,128)(2,1)}) fusion(bf16[2,256,3,64]{1,3,2,0:T(8,128)(2,1)} %bitcast.138, f32[2,3,256,256]{2,3,1,0:T(8,128)} %fusion.60, f32[2,3,256,256]{2,3,1,0:T(8,128)S(1)} %get-tuple-element.105, f32[2,3,256]{2,1,0:T(4,128)S(1)} %copy-done.23), kind=kOutput, calls=%fused_computation.167 | convolution fusion | flops 53282368 | bytes 3545856 | tf_op jit(solution)/shard_map/lhqk,lkhe->lqhe/dot_general | solution.py:49
  170.4 3.4 %fusion.34 = bf16[2,3,64,256]{3,2,1,0:T(8,128)(2,1)} fusion(f32[2,3,256,256]{2,3,1,0:T(8,128)} %fusion.60, f32[2,3,256,256]{2,3,1,0:T(8,128)S(1)} %get-tuple-element.105, f32[2,3,256]{2,1,0:T(4,128)S(1)} %copy-done.23, f32[2,256,3,64]{1,3,2,0:T(8,128)} %bitcast.131, f32[3,64]{1,0:T(4,128)S(1)} %copy-done.46), kind=kOutput, calls=%fused_computation.59 | convolution fusion | flops 53380864 | bytes 3742464 | tf_op jit(solution)/shard_map/lhqk,lqhe->lkhe/dot_general | solution.py:49
  176.4 2.2 concatenate.14
  178.7 2.2 copy.52
  180.9 2.0 fusion.26
  185.4 1.7 bitcast_convert_fusion.3.refs_0_
  187.1 26.5 %shard_map.242 = (bf16[3,2,64,768]{3,2,1,0:T(8,128)(2,1)}, bf16[7,96,768]{2,1,0:T(8,128)(2,1)}) custom-call(bf16[2,256,768]{2,1,0:T(8,128)(2,1)} %bitcast_convert_fusion.3.refs_0_, bf16[8,96,768]{2,1,0:T(8,128)(2,1)} %pad_maximum_fusion.refs_1_), custom_call_target="tpu_custom_call" | custom-call | tf_op jit(solution)/shard_map/pallas_call | solution.py:132
  222.2 1.8 add_convert_fusion.1.refs_0_
  224.0 23.4 %shard_map.243 = (bf16[2,256,768]{2,1,0:T(8,128)(2,1)}, f32[4,13,768]{2,1,0:T(8,128)}) custom-call(bf16[2,64,768]{2,1,0:T(8,128)(2,1)} %add_convert_fusion.1.refs_0_, f32[13,768]{1,0:T(8,128)} %pad_maximum_fusion.4.refs_1_), custom_call_target="tpu_custom_call" | custom-call | tf_op jit(solution)/shard_map/pallas_call | solution.py:132
  248.5 1.5 fusion.18
  251.8 10.6 %shard_map.244 = (f32[8,1,4992]{2,1,0:T(1,128)}, f32[4,2,768]{2,1,0:T(2,128)}) custom-call(f32[1,4992]{1,0:T(1,128)} %broadcast_in_dim.8.refs_0_, f32[2,768]{1,0:T(2,128)} %fusion.72.refs_1_), custom_call_target="tpu_custom_call" | custom-call | tf_op jit(solution)/shard_map/pallas_call | solution.py:132
  (217 shorter events, 44.2 us)
Async XLA Ops:
  0.7 3.1 %copy-start.29 = (bf16[2,768]{1,0:T(2,128)(2,1)S(1)}, bf16[2,768]{1,0:T(2,128)(2,1)}, u32[]{:S(2)}) copy-start(bf16[2,768]{1,0:T(2,128)(2,1)} %param.15) | copy-start | bytes 9220
  0.7 14.8 %copy-start.1 = (bf16[2,256,768]{2,1,0:T(8,128)(2,1)S(1)}, bf16[2,256,768]{2,1,0:T(8,128)(2,1)}, u32[]{:S(2)}) copy-start(bf16[2,256,768]{2,1,0:T(8,128)(2,1)} %param.14) | copy-start | bytes 2359300
  0.7 15.4 %copy-start.58 = (bf16[768,3,192]{0,2,1:T(8,128)(2,1)S(1)}, bf16[768,3,192]{0,2,1:T(8,128)(2,1)}, u32[]{:S(2)}) copy-start(bf16[768,3,192]{0,2,1:T(8,128)(2,1)} %param.19) | copy-start | bytes 2654212
  18.0 3.0 %copy-start.15 = (bf16[2,256,1,192]{1,3,2,0:T(8,128)(2,1)}, bf16[2,256,1,192]{1,3,2,0:T(8,128)(2,1)S(1)}, u32[]{:S(2)}) copy-start(bf16[2,256,1,192]{1,3,2,0:T(8,128)(2,1)S(1)} %slice.108) | copy-start | bytes 589828
  22.3 3.4 %copy-start.39 = (f32[3,64]{1,0:T(4,128)}, f32[3,64]{1,0:T(4,128)S(1)}, u32[]{:S(2)}) copy-start(f32[3,64]{1,0:T(4,128)S(1)} %add.225) | copy-start | bytes 2308
  43.2 3.2 %copy-start.41 = (f32[768]{0:T(1024)S(1)}, f32[768]{0:T(1024)}, u32[]{:S(2)}) copy-start(f32[768]{0:T(1024)} %param.22) | copy-start | bytes 9220
  45.2 3.2 %copy-start.31 = (f32[2,768]{1,0:T(2,128)S(1)}, f32[2,768]{1,0:T(2,128)}, u32[]{:S(2)}) copy-start(f32[2,768]{1,0:T(2,128)} %get-tuple-element.96) | copy-start | bytes 18436
  46.5 22.0 %copy-start.60 = (f32[768]{0:T(1024)S(1)}, f32[768]{0:T(1024)}, u32[]{:S(2)}) copy-start(f32[768]{0:T(1024)} %param.24) | copy-start | bytes 9220
  68.5 3.1 %copy-start.13 = (bf16[2,256,768]{2,1,0:T(8,128)(2,1)S(1)}, bf16[2,256,768]{2,1,0:T(8,128)(2,1)}, u32[]{:S(2)}) copy-start(bf16[2,256,768]{2,1,0:T(8,128)(2,1)} %param.27) | copy-start | bytes 2359300
  68.6 3.1 %copy-start.26 = (f32[2,768]{1,0:T(2,128)S(1)}, f32[2,768]{1,0:T(2,128)}, u32[]{:S(2)}) copy-start(f32[2,768]{1,0:T(2,128)} %get-tuple-element.95) | copy-start | bytes 18436
  68.6 3.1 %copy-start.57 = (bf16[768,768]{1,0:T(8,128)(2,1)S(1)}, bf16[768,768]{1,0:T(8,128)(2,1)}, u32[]{:S(2)}) copy-start(bf16[768,768]{1,0:T(8,128)(2,1)} %param.25) | copy-start | bytes 3538948
  71.7 52.4 %copy-start.54 = (f32[2]{0:T(128)}, f32[2]{0:T(128)S(1)}, u32[]{:S(2)}) copy-start(f32[2]{0:T(128)S(1)} %compare_convert_fusion) | copy-start | bytes 28
  117.4 3.6 %copy-start.20 = (bf16[3,2,64,768]{3,2,1,0:T(8,128)(2,1)S(1)}, bf16[3,2,64,768]{3,2,1,0:T(8,128)(2,1)}, u32[]{:S(2)}) copy-start(bf16[3,2,64,768]{3,2,1,0:T(8,128)(2,1)} %get-tuple-element.28) | copy-start | bytes 1769476
  117.4 4.9 %copy-start.5 = (f32[2,64,768]{2,1,0:T(8,128)S(1)}, f32[2,64,768]{2,1,0:T(8,128)}, u32[]{:S(2)}) copy-start(f32[2,64,768]{2,1,0:T(8,128)} %copy-done.4) | copy-start | bytes 1179652
  120.9 3.2 %copy-start.10 = (f32[2,64,768]{2,1,0:T(8,128)S(1)}, f32[2,64,768]{2,1,0:T(8,128)}, u32[]{:S(2)}) copy-start(f32[2,64,768]{2,1,0:T(8,128)} %convert_reduce_fusion.6) | copy-start | bytes 1179652
  120.9 3.2 %copy-start.50 = (f32[768]{0:T(1024)S(1)}, f32[768]{0:T(1024)}, u32[]{:S(2)}) copy-start(f32[768]{0:T(1024)} %param.26) | copy-start | bytes 9220
  126.9 36.7 %copy-start.40 = (f32[3,64]{1,0:T(4,128)S(1)}, f32[3,64]{1,0:T(4,128)}, u32[]{:S(2)}) copy-start(f32[3,64]{1,0:T(4,128)} %copy-done.39) | copy-start | bytes 2308
  162.0 4.4 %copy-start.23 = (f32[2,3,256]{2,1,0:T(4,128)S(1)}, f32[2,3,256]{2,1,0:T(4,128)}, u32[]{:S(2)}) copy-start(f32[2,3,256]{2,1,0:T(4,128)} %log_add_fusion) | copy-start | bytes 18436
  166.4 3.9 %copy-start.46 = (f32[3,64]{1,0:T(4,128)S(1)}, f32[3,64]{1,0:T(4,128)}, u32[]{:S(2)}) copy-start(f32[3,64]{1,0:T(4,128)} %add.228) | copy-start | bytes 2308
  215.2 3.4 %copy-start.3 = (bf16[2,256,768]{2,1,0:T(8,128)(2,1)S(1)}, bf16[2,256,768]{2,1,0:T(8,128)(2,1)}, u32[]{:S(2)}) copy-start(bf16[2,256,768]{2,1,0:T(8,128)(2,1)} %param.14) | copy-start | bytes 2359300
  215.2 3.4 %copy-start.38 = (f32[2,256]{1,0:T(2,128)S(1)}, f32[2,256]{1,0:T(2,128)}, u32[]{:S(2)}) copy-start(f32[2,256]{1,0:T(2,128)} %copy-done.36) | copy-start | bytes 6148
  215.2 3.4 %copy-start.45 = (f32[2,256]{1,0:T(2,128)S(1)}, f32[2,256]{1,0:T(2,128)}, u32[]{:S(2)}) copy-start(f32[2,256]{1,0:T(2,128)} %copy-done.43) | copy-start | bytes 6148
  218.6 2.8 %copy-start.32 = (f32[2,768]{1,0:T(2,128)S(1)}, f32[2,768]{1,0:T(2,128)}, u32[]{:S(2)}) copy-start(f32[2,768]{1,0:T(2,128)} %get-tuple-element.69) | copy-start | bytes 18436
  218.6 2.9 %copy-start.42 = (f32[768]{0:T(1024)S(1)}, f32[768]{0:T(1024)}, u32[]{:S(2)}) copy-start(f32[768]{0:T(1024)} %get-tuple-element.86) | copy-start | bytes 9220
  218.6 3.6 %copy-start.8 = (f32[2,64,768]{2,1,0:T(8,128)S(1)}, f32[2,64,768]{2,1,0:T(8,128)}, u32[]{:S(2)}) copy-start(f32[2,64,768]{2,1,0:T(8,128)} %copy-done.7) | copy-start | bytes 1179652
  220.1 28.4 %copy-start.51 = (f32[768]{0:T(1024)S(1)}, f32[768]{0:T(1024)}, u32[]{:S(2)}) copy-start(f32[768]{0:T(1024)} %get-tuple-element.108) | copy-start | bytes 9220
  221.2 27.3 %copy-start.27 = (f32[2,768]{1,0:T(2,128)S(1)}, f32[2,768]{1,0:T(2,128)}, u32[]{:S(2)}) copy-start(f32[2,768]{1,0:T(2,128)} %get-tuple-element.95) | copy-start | bytes 18436
  221.2 27.3 %copy-start.55 = (f32[2]{0:T(128)S(1)}, f32[2]{0:T(128)}, u32[]{:S(2)}) copy-start(f32[2]{0:T(128)} %copy-done.54) | copy-start | bytes 28
  248.5 15.5 %copy-start.28 = (f32[8,2,768]{2,1,0:T(2,128)S(1)}, f32[8,2,768]{2,1,0:T(2,128)}, u32[]{:S(2)}) copy-start(f32[8,2,768]{2,1,0:T(2,128)} %get-tuple-element.36) | copy-start | bytes 147460
  250.6 18.1 %copy-start.30 = (bf16[2,768]{1,0:T(2,128)(2,1)S(1)}, bf16[2,768]{1,0:T(2,128)(2,1)}, u32[]{:S(2)}) copy-start(bf16[2,768]{1,0:T(2,128)(2,1)} %param.15) | copy-start | bytes 9220
  250.7 18.7 %copy-start.17 = (bf16[2,256,768]{2,1,0:T(8,128)(2,1)S(1)}, bf16[2,256,768]{2,1,0:T(8,128)(2,1)}, u32[]{:S(2)}) copy-start(bf16[2,256,768]{2,1,0:T(8,128)(2,1)} %get-tuple-element.33) | copy-start | bytes 2359300
  264.1 6.5 %copy-start.16 = (bf16[2,256,768]{2,1,0:T(8,128)(2,1)S(1)}, bf16[2,256,768]{2,1,0:T(8,128)(2,1)}, u32[]{:S(2)}) copy-start(bf16[2,256,768]{2,1,0:T(8,128)(2,1)} %get-tuple-element.129) | copy-start | bytes 2359300
  (33 other events, 54.2 us)

commit v2 on v1

--- a/solution.py
+++ b/solution.py
@@ -143,6 +143,33 @@
     )(*[array for _, _, array in items])
 
 
+def shift_tensor(array, step):
+    size = lax.axis_size("tensor")
+    return lax.ppermute(array, "tensor", [(i, (i + step) % size) for i in range(size)])
+
+
+def scatter_async(piece, rows):
+    size, index = lax.axis_size("tensor"), lax.axis_index("tensor")
+    parts = [
+        shift_tensor(
+            lax.dynamic_slice_in_dim(piece, lax.rem(index + step, size) * rows, rows, 1), step
+        )
+        for step in range(1, size)
+    ]
+    own = lax.dynamic_slice_in_dim(piece, index * rows, rows, 1)
+    return sum(part.astype(jnp.float32) for part in [own] + parts)
+
+
+def place_rows(parts):
+    size, index = len(parts), lax.axis_index("tensor")
+    rows = parts[0].shape[1]
+    whole = jnp.zeros(parts[0].shape[:1] + (rows * size,) + parts[0].shape[2:], parts[0].dtype)
+    for step, part in enumerate(parts):
+        source = lax.rem(index - step + size, size)
+        whole = lax.dynamic_update_slice_in_dim(whole, part, source * rows, 1)
+    return whole
+
+
 def sum_rows(piece, arrived, start):
     own = lax.dynamic_slice_in_dim(piece, start, arrived.shape[2], 1).astype(jnp.float32)
     return own + jnp.sum(arrived.astype(jnp.float32), axis=0)
@@ -216,6 +243,7 @@
     preactivation_rows = contract_lowprec("kow,wz->koz", hidden_second, dense1_weight) + dense1_bias
     activation_lowprec = to_half(jax.nn.gelu(preactivation_rows, approximate=True))
     perceptron_piece = to_half(contract_lowprec("jqv,vg->jqg", activation_lowprec, dense2_weight))
+    perceptron_sum = scatter_async(perceptron_piece, rows_dev)
     dmlp = gate_two * (live_mask * cotangent.astype(jnp.float32))
     perceptron_gradient_lowprec = to_half(dmlp)
     grad_fc2_part = jnp.sum(dmlp, axis=(0, 1))
@@ -234,21 +262,15 @@
     hidden_gradient_piece = to_half(
         contract_lowprec("hnb,jb->hnj", preactivation_gradient_lowprec, dense1_weight)
     )
-    hidden_arrived, perceptron_arrived, fc1_arrived, fc2_arrived = exchange(
+    hidden_arrived, fc1_arrived = exchange(
         4,
         ("tensor", "scatter_rows", hidden_gradient_piece),
-        ("tensor", "scatter_rows", perceptron_piece),
         ("dp", "scatter", dense1_gradient),
-        ("dp", "scatter", dense2_gradient),
     )
     summed_fc1 = sum_blocks(dense1_gradient, fc1_arrived, dp_index)
-    summed_fc2 = sum_blocks(dense2_gradient, fc2_arrived, dp_index).T
     hidden_second_gradient = sum_rows(hidden_gradient_piece, hidden_arrived, row_start)
-    perceptron_branch = sum_rows(perceptron_piece, perceptron_arrived, row_start) + dense2_bias
-    output_own = to_half(live_mask * (x_one + gate_two * perceptron_branch))
     cot_own = lax.dynamic_slice_in_dim(cotangent, row_start, rows_dev, 1)
     grad_out = live_mask * cot_own.astype(jnp.float32)
-    dgate_two = jnp.sum(grad_out * perceptron_branch, axis=1)
     dscale_two = jnp.sum(hidden_second_gradient * norm_two, axis=1)
     dshift_two = jnp.sum(hidden_second_gradient, axis=1)
     dx_one = grad_out + norm_back(hidden_second_gradient * (1.0 + scale_two), norm_two, recip_two)
@@ -256,9 +278,15 @@
     dgate_one = jnp.sum(dx_one * attn_branch, axis=1)
     dattn_own_b = to_half(dattn)
     grad_proj_part = jnp.sum(dattn, axis=(0, 1))
-    dattn_b, block_output = exchange(
-        5, ("tensor", "gather_rows", dattn_own_b), ("tensor", "gather_rows", output_own)
-    )
+    dattn_b, fc2_arrived = exchange(
+        5, ("tensor", "gather_rows", dattn_own_b), ("dp", "scatter", dense2_gradient)
+    )
+    summed_fc2 = sum_blocks(dense2_gradient, fc2_arrived, dp_index).T
+    perceptron_branch = perceptron_sum + dense2_bias
+    output_own = to_half(live_mask * (x_one + gate_two * perceptron_branch))
+    dgate_two = jnp.sum(grad_out * perceptron_branch, axis=1)
+    output_own, dattn_b = lax.optimization_barrier((output_own, dattn_b))
+    parts = [output_own] + [shift_tensor(output_own, step) for step in range(1, tensor_count)]
     grad_proj = contract_lowprec("lse,lsd->ed", dattn_b, attended)
     dattended = to_half(contract_lowprec("lse,de->lsd", dattn_b, proj_weight)).reshape(
         lat_cap, seq_len, head_count, HD
@@ -269,6 +297,7 @@
     dprobs = contract_lowprec("lqhe,lkhe->lhqk", dattended, value_rows)
     delta = jnp.sum(probs * dprobs, axis=-1, keepdims=True)
     dscores_b = to_half(probs * (dprobs - delta) * scale_qk)
+    parts[1 % tensor_count], dscores_b = lax.optimization_barrier((parts[1 % tensor_count], dscores_b))
     dquery = contract_lowprec("lhqk,lkhe->lqhe", dscores_b, key_rows).reshape(
         lat_cap, seq_len, local_width
     )
@@ -280,8 +309,11 @@
     )
     grad_qv = jnp.stack([jnp.sum(dquery, axis=(0, 1)), jnp.sum(dvalue, axis=(0, 1))], axis=0)
     dqkv_b = to_half(jnp.stack([dquery, dkey, dvalue], axis=2))
+    parts[2 % tensor_count], dqkv_b = lax.optimization_barrier((parts[2 % tensor_count], dqkv_b))
     grad_qkv = contract_lowprec("lsd,lsce->dce", h_one, dqkv_b)
     dh_part_one = to_half(contract_lowprec("lsce,dce->lsd", dqkv_b, qkv_weight))
+    parts[3 % tensor_count], dh_part_one = lax.optimization_barrier((parts[3 % tensor_count], dh_part_one))
+    block_output = place_rows(parts)
     attn_gradient = jnp.concatenate(
         [to_half(grad_qkv).reshape(width, 3 * local_width), to_half(grad_proj)], axis=1
     ).reshape(dp_count, width // dp_count, 4 * local_width)
@@ -315,7 +347,7 @@
     col_start = tensor_index * local_cols
     dmod_local = lax.dynamic_slice_in_dim(dmod, col_start, local_cols, 1)
     cond_part = contract_lowprec("le,de->ld", to_half(dmod_local), ada_weight)
-    parts = [
+    vectors = [
         dmod_local.reshape(-1),
         grad_qv.reshape(-1),
         grad_fc1_b,
@@ -323,7 +355,7 @@
         stats_sum[lat_cap * 6],
     ]
     packed_all, cond_all = exchange(
-        8, ("dp", "gather", jnp.concatenate(parts)[None]), ("tensor", "gather", cond_part)
+        8, ("dp", "gather", jnp.concatenate(vectors)[None]), ("tensor", "gather", cond_part)
     )
     grad_conditioning = jnp.sum(cond_all, axis=0) * silu_slope(cond_f)
     packed_all = packed_all[:, 0]

time: 272 us -> 265 us (0.974)
  Pallas kernels: 174 us -> 138 us
  starting transfers between devices: 0 us -> 12.2 us
  local copies, waits for them, and re-layouts: 20.9 us -> 30.4 us
  other arithmetic: 36 us -> 40.9 us
    pallas_call x8, Pallas kernels: 174 us -> 138 us  [exchange(): pl.pallas_call(functools.partial(exchange_body, kinds, sizes, copy_count)...]
    ppermute x0 -> x6, starting transfers between devices: none -> 12.2 us  [shift_tensor(): lax.ppermute(array, 'tensor', [(i, (i + step) % size) for i in range(size)])]
    dot_general x20 -> x19, matrix products: 36.7 us -> 32.7 us  [contract_lowprec(): return jnp.einsum(form, left, right, preferred_element_type=jnp.float32)]
    sub x0 -> x1, matrix products: none -> 3.09 us  [per_device(): dscores_b = to_half(probs * (dprobs - delta) * scale_qk)]
    dynamic_update_slice x0 -> x4, local copies, waits for them, and re-layouts: none -> 2.86 us  [place_rows(): whole = lax.dynamic_update_slice_in_dim(whole, part, source * rows, 1)]
    unnamed x138 -> x151, local copies, waits for them, and re-layouts: 9.68 us -> 7.81 us
  transfers between devices with their start and end apart: 0 -> 6, of which waited for: 0 -> 1; matrix products, arithmetic and copies ran while one was open for 0% -> 15% of each run, Pallas kernels for 0% -> 6%
where the time goes in v2:
time: 265 us; the launch traced here: 264 us
  Pallas kernels  138 us (52%)
  other arithmetic  40.9 us (15%)
  matrix products  37.5 us (14%)
  local copies, waits for them, and re-layouts  30.4 us (11%)
  starting transfers between devices  12.2 us (5%)
    pallas_call x8, Pallas kernels, exchange(): pl.pallas_call(functools.partial(exchange_body, kinds, sizes, copy_count)...  138 us
    dot_general x19, matrix products, contract_lowprec(): return jnp.einsum(form, left, right, preferred_element_type=jnp.float32)  32.7 us
    ppermute x6, starting transfers between devices, shift_tensor(): lax.ppermute(array, 'tensor', [(i, (i + step) % size) for i in range(size)])  12.2 us
    unnamed x151, local copies, waits for them, and re-layouts  7.81 us
  transfers between devices with their start and end apart: 6, of which 1 were waited for; matrix products, arithmetic and copies ran while one was open for 15% of the time, Pallas kernels for 6%

profile of v2, /device:TPU:0, one launch (start us, length us, event | category | flops | bytes accessed | tf_op | source)
XLA Modules:
  0.0 264.0 jit_solution(13610211273025783617)
XLA Ops:
  3.9 9.7 %shard_map.237 = (f32[4,2,1152]{2,1,0:T(2,128)}, f32[8,2,768]{2,1,0:T(2,128)}) custom-call(f32[2,1152]{1,0:T(2,128)} %convolution_add_fusion.refs_0_, f32[2,768]{1,0:T(2,128)} %fusion.57.refs_1_), custom_call_target="tpu_custom_call" | custom-call | tf_op jit(solution)/shard_map/pallas_call | solution.py:132
  27.1 17.5 %shard_map.238 = bf16[3,2,64,768]{3,2,1,0:T(8,128)(2,1)} custom-call(bf16[2,256,768]{2,1,0:T(8,128)(2,1)} %convolution_convert_fusion.2.refs_0_), custom_call_target="tpu_custom_call" | custom-call | tf_op jit(solution)/shard_map/pallas_call | solution.py:132
  44.6 1.9 convert_reduce_fusion.5
  49.5 19.3 %shard_map.239 = bf16[2,256,768]{2,1,0:T(8,128)(2,1)} custom-call(bf16[2,64,768]{2,1,0:T(8,128)(2,1)} %add_convert_fusion.2.refs_0_), custom_call_target="tpu_custom_call" | custom-call | tf_op jit(solution)/shard_map/pallas_call | solution.py:132
  68.9 2.4 convolution_add_fusion.1
  72.4 2.0 convolution_convert_fusion.1
  74.4 1.9 constant_dynamic-slice_fusion.5
  76.3 3.7 %collective-permute-start = (bf16[2,64,768]{2,1,0:T(8,128)(2,1)}, bf16[2,64,768]{2,1,0:T(8,128)(2,1)}, u32[]{:S(2)}, u32[]{:S(2)}) collective-permute-start(bf16[2,64,768]{2,1,0:T(8,128)(2,1)} %get-tuple-element.100), channel_id=1, source_target_pairs={{0,1},{1,2},{2,3},{3,0},{4,5},{5,6},{6,7},{7,4},{8,9},{9,10},{10,1... | collective-permute-start | bytes 589832 | tf_op jit(solution)/shard_map/ppermute | solution.py:148
  80.0 2.1 collective-permute-start.1
  83.1 4.2 %fusion.68 = (f32[768]{0:T(1024)}, bf16[2,256,768]{2,1,0:T(8,128)(2,1)S(1)}) fusion(f32[2,256,768]{2,1,0:T(8,128)} %copy-done.70, bf16[768,768]{1,0:T(8,128)(2,1)} %param.25, bf16[2,256,768]{2,1,0:T(8,128)(2,1)} %param.27, f32[2]{0:T(128)S(1)} %compare_convert_fusion, f32[2,768]{1,0:T(2,128)} %get-tuple-element.114), kind=kOutput, calls=%fused_computation.166 | convolution fusion | flops 613416192 | bytes 4334600 | tf_op jit(solution)/shard_map/vug,bg->vub/dot_general | solution.py:49
  87.3 1.9 bitcast_convert_fusion.1
  90.9 2.1 bitcast_convert_fusion
  94.5 17.0 %shard_map.240 = (bf16[3,2,64,768]{3,2,1,0:T(8,128)(2,1)}, bf16[7,96,768]{2,1,0:T(8,128)(2,1)}) custom-call(bf16[2,256,768]{2,1,0:T(8,128)(2,1)} %convolution_convert_fusion.refs_0_, bf16[8,96,768]{2,1,0:T(8,128)(2,1)} %bitcast.131), custom_call_target="tpu_custom_call" | custom-call | tf_op jit(solution)/shard_map/pallas_call | solution.py:132
  111.5 1.9 convert_reduce_fusion.4
  113.4 2.1 convert_reduce_fusion.1
  121.4 2.1 fusion.18
  123.5 3.4 %multiply_reduce_fusion.2 = (f32[2,768]{1,0:T(2,128)}, bf16[2,64,768]{2,1,0:T(8,128)(2,1)}, f32[2,768]{1,0:T(2,128)}, f32[2,64]{1,0:T(2,128)S(1)}, f32[2,64]{1,0...) fusion(f32[2]{0:T(128)} %copy-done.61, bf16[2,256,768]{2,1,0:T(8,128)(2,1)} %param.27, s32[]{:T(128)S(6)} %select_n.48, ...), kind=kLoop, calls=%fused_computation.69 | loop fusion | flops 2649344 | bytes 2591756 | tf_op jit(solution)/shard_map/reduce_sum | solution.py:287
  127.0 1.9 multiply_reduce_fusion.4
  130.4 21.7 %shard_map.241 = (bf16[2,256,768]{2,1,0:T(8,128)(2,1)}, bf16[7,96,768]{2,1,0:T(8,128)(2,1)}) custom-call(bf16[2,64,768]{2,1,0:T(8,128)(2,1)} %multiply_convert_fusion.2.refs_0_, bf16[8,96,768]{2,1,0:T(8,128)(2,1)} %bitcast.129), custom_call_target="tpu_custom_call" | custom-call | tf_op jit(solution)/shard_map/pallas_call | solution.py:132
  152.1 2.3 convolution_convert_fusion.4
  154.4 3.1 %multiply_convert_fusion = bf16[2,3,256,256]{2,3,1,0:T(8,128)(2,1)} fusion(f32[2,3,256,256]{2,3,1,0:T(8,128)S(1)} %get-tuple-element.122, f32[2,3,256]{2,1,0:T(4,128)S(1)} %copy-done.27, bf16[2,256,3,64]{1,3,2,0:T(8,128)(2,1)} %bitcast.135, f32[2,256,3,64]{1,3,2,0:T(8,128)} %bitcast.128, f32[3,64]{1,0:T(4,128)S(1)} %copy-done.56), kind=kOutput, calls=%fused_computation.26 | convolution fusion | flops 103810816 | bytes 2956032 | tf_op jit(solution)/shard_map/sub | solution.py:299
  157.5 2.7 %fusion.65 = (f32[3,64]{1,0:T(4,128)}, bf16[2,256,3,64]{1,3,2,0:T(8,128)(2,1)}) fusion(bf16[2,256,3,64]{1,3,2,0:T(8,128)(2,1)} %bitcast.136, f32[2,3,256,256]{2,3,1,0:T(8,128)S(1)} %get-tuple-element.122, f32[2,3,256]{2,1,0:T(4,128)S(1)} %copy-done.27), kind=kOutput, calls=%fused_computation.163 | convolution fusion | flops 51314496 | bytes 1972992 | tf_op jit(solution)/shard_map/lhqk,lqhe->lkhe/dot_general | solution.py:49
  160.1 3.3 %collective-permute-start.3 = (bf16[2,64,768]{2,1,0:T(8,128)(2,1)}, bf16[2,64,768]{2,1,0:T(8,128)(2,1)S(1)}, u32[]{:S(2)}, u32[]{:S(2)}) collective-permute-start(bf16[2,64,768]{2,1,0:T(8,128)(2,1)} %get-tuple-element.36), channel_id=1, source_target_pairs={{0,1},{1,2},{2,3},{3,0},{4,5},{5,6},{6,7},{7,4},{8,9},{9,10},{10,1... | collective-permute-start | bytes 589832 | tf_op jit(solution)/shard_map/ppermute | solution.py:148
  163.5 2.5 collective-permute-start.4
  172.3 1.9 fusion.34
  175.7 2.4 collective-permute-done.4
  179.0 2.2 concatenate.14
  181.2 2.1 copy.46
  183.4 3.0 %bitcast_convert_fusion.3.refs_0_ = bf16[2,256,768]{2,1,0:T(8,128)(2,1)} fusion(bf16[2,256,3,192]{1,3,0,2:T(8,128)(2,1)} %copy-done.23, bf16[768,3,192]{0,2,1:T(8,128)(2,1)} %param.19), kind=kOutput, calls=%fused_computation.25 | convolution fusion | flops 453378048 | bytes 2260992 | tf_op jit(solution)/shard_map/lsce,dce->lsd/dot_general | solution.py:49
  187.6 20.5 %shard_map.242 = (bf16[3,2,64,768]{3,2,1,0:T(8,128)(2,1)}, bf16[7,96,768]{2,1,0:T(8,128)(2,1)}) custom-call(bf16[2,256,768]{2,1,0:T(8,128)(2,1)} %bitcast_convert_fusion.3.refs_0_, bf16[8,96,768]{2,1,0:T(8,128)(2,1)} %pad_maximum_fusion.refs_1_), custom_call_target="tpu_custom_call" | custom-call | tf_op jit(solution)/shard_map/pallas_call | solution.py:132
  214.8 23.3 %shard_map.243 = (bf16[2,256,768]{2,1,0:T(8,128)(2,1)}, f32[4,13,768]{2,1,0:T(8,128)}) custom-call(bf16[2,64,768]{2,1,0:T(8,128)(2,1)} %add_convert_fusion.1.refs_0_, f32[13,768]{1,0:T(8,128)} %pad_maximum_fusion.2.refs_1_), custom_call_target="tpu_custom_call" | custom-call | tf_op jit(solution)/shard_map/pallas_call | solution.py:132
  241.2 9.3 %shard_map.244 = (f32[8,1,4992]{2,1,0:T(1,128)}, f32[4,2,768]{2,1,0:T(2,128)}) custom-call(f32[1,4992]{1,0:T(1,128)} %broadcast_in_dim.11.refs_0_, f32[2,768]{1,0:T(2,128)} %fusion.55.refs_1_), custom_call_target="tpu_custom_call" | custom-call | tf_op jit(solution)/shard_map/pallas_call | solution.py:132
  (250 shorter events, 64.1 us)
Async XLA Ops:
  0.7 14.3 %copy-start.1 = (bf16[2,256,768]{2,1,0:T(8,128)(2,1)S(1)}, bf16[2,256,768]{2,1,0:T(8,128)(2,1)}, u32[]{:S(2)}) copy-start(bf16[2,256,768]{2,1,0:T(8,128)(2,1)} %param.14) | copy-start | bytes 2359300
  2.1 13.4 %copy-start.69 = (bf16[768,3,192]{0,2,1:T(8,128)(2,1)S(1)}, bf16[768,3,192]{0,2,1:T(8,128)(2,1)}, u32[]{:S(2)}) copy-start(bf16[768,3,192]{0,2,1:T(8,128)(2,1)} %param.19) | copy-start | bytes 2654212
  76.3 47.2 %collective-permute-start = (bf16[2,64,768]{2,1,0:T(8,128)(2,1)}, bf16[2,64,768]{2,1,0:T(8,128)(2,1)}, u32[]{:S(2)}, u32[]{:S(2)}) collective-permute-start(bf16[2,64,768]{2,1,0:T(8,128)(2,1)} %get-tuple-element.100), channel_id=1, source_target_pairs={{0,1},{1,2},{2,3},{3,0},{4,5},{5,6},{6,7},{7,4},{8,9},{9,10},{10,1... | collective-permute-start | bytes 589832 | tf_op jit(solution)/shard_map/ppermute | solution.py:148
  80.0 43.5 %collective-permute-start.1 = (bf16[2,64,768]{2,1,0:T(8,128)(2,1)}, bf16[2,64,768]{2,1,0:T(8,128)(2,1)}, u32[]{:S(2)}, u32[]{:S(2)}) collective-permute-start(bf16[2,64,768]{2,1,0:T(8,128)(2,1)} %get-tuple-element.102), channel_id=1, source_target_pairs={{0,2},{1,3},{2,0},{3,1},{4,6},{5,7},{6,4},{7,5},{8,10},{9,11},{10,... | collective-permute-start | bytes 589832 | tf_op jit(solution)/shard_map/ppermute | solution.py:148
  82.2 41.3 %collective-permute-start.2 = (bf16[2,64,768]{2,1,0:T(8,128)(2,1)}, bf16[2,64,768]{2,1,0:T(8,128)(2,1)}, u32[]{:S(2)}, u32[]{:S(2)}) collective-permute-start(bf16[2,64,768]{2,1,0:T(8,128)(2,1)} %get-tuple-element.101), channel_id=1, source_target_pairs={{0,3},{1,0},{2,1},{3,2},{4,7},{5,4},{6,5},{7,6},{8,11},{9,8},{10,9... | collective-permute-start | bytes 589832 | tf_op jit(solution)/shard_map/ppermute | solution.py:148
  83.1 7.8 %copy-start.61 = (f32[2]{0:T(128)}, f32[2]{0:T(128)S(1)}, u32[]{:S(2)}) copy-start(f32[2]{0:T(128)S(1)} %compare_convert_fusion) | copy-start | bytes 28
  121.3 5.6 %copy-start.33 = (f32[2,64]{1,0:T(2,128)S(1)}, f32[2,64]{1,0:T(2,128)}, u32[]{:S(2)}) copy-start(f32[2,64]{1,0:T(2,128)} %copy-done.32) | copy-start | bytes 1540
  121.4 5.6 %copy-start.47 = (f32[768]{0:T(1024)S(1)}, f32[768]{0:T(1024)}, u32[]{:S(2)}) copy-start(f32[768]{0:T(1024)} %param.22) | copy-start | bytes 9220
  121.4 5.6 %copy-start.49 = (f32[2,64]{1,0:T(2,128)S(1)}, f32[2,64]{1,0:T(2,128)}, u32[]{:S(2)}) copy-start(f32[2,64]{1,0:T(2,128)} %copy-done.48) | copy-start | bytes 1540
  121.4 5.6 %copy-start.62 = (f32[2]{0:T(128)S(1)}, f32[2]{0:T(128)}, u32[]{:S(2)}) copy-start(f32[2]{0:T(128)} %copy-done.61) | copy-start | bytes 28
  129.7 24.7 %copy-start.27 = (f32[2,3,256]{2,1,0:T(4,128)S(1)}, f32[2,3,256]{2,1,0:T(4,128)}, u32[]{:S(2)}) copy-start(f32[2,3,256]{2,1,0:T(4,128)} %log_add_fusion) | copy-start | bytes 18436
  130.4 24.0 %copy-start.56 = (f32[3,64]{1,0:T(4,128)S(1)}, f32[3,64]{1,0:T(4,128)}, u32[]{:S(2)}) copy-start(f32[3,64]{1,0:T(4,128)} %add.270) | copy-start | bytes 2308
  157.5 8.5 %copy-start.10 = (bf16[2,256,768]{2,1,0:T(8,128)(2,1)S(1)}, bf16[2,256,768]{2,1,0:T(8,128)(2,1)}, u32[]{:S(2)}) copy-start(bf16[2,256,768]{2,1,0:T(8,128)(2,1)} %get-tuple-element.37) | copy-start | bytes 2359300
  157.5 8.5 %copy-start.13 = (bf16[2,3,64,256]{3,2,1,0:T(8,128)(2,1)S(1)}, bf16[2,3,64,256]{3,2,1,0:T(8,128)(2,1)}, u32[]{:S(2)}) copy-start(bf16[2,3,64,256]{3,2,1,0:T(8,128)(2,1)} %copy-done.12) | copy-start | bytes 589828
  157.5 11.1 %copy-start.38 = (f32[2,768]{1,0:T(2,128)S(1)}, f32[2,768]{1,0:T(2,128)}, u32[]{:S(2)}) copy-start(f32[2,768]{1,0:T(2,128)} %get-tuple-element.96) | copy-start | bytes 18436
  160.1 6.6 %copy-start.58 = (f32[3,64]{1,0:T(4,128)S(1)}, f32[3,64]{1,0:T(4,128)}, u32[]{:S(2)}) copy-start(f32[3,64]{1,0:T(4,128)} %get-tuple-element.110) | copy-start | bytes 2308
  160.1 7.2 %copy-start.41 = (f32[2,768]{1,0:T(2,128)S(1)}, f32[2,768]{1,0:T(2,128)}, u32[]{:S(2)}) copy-start(f32[2,768]{1,0:T(2,128)} %get-tuple-element.86) | copy-start | bytes 18436
  160.1 7.2 %copy-start.40 = (f32[2,768]{1,0:T(2,128)S(1)}, f32[2,768]{1,0:T(2,128)}, u32[]{:S(2)}) copy-start(f32[2,768]{1,0:T(2,128)} %get-tuple-element.103) | copy-start | bytes 18436
  160.1 7.8 %copy-start.39 = (f32[2,768]{1,0:T(2,128)S(1)}, f32[2,768]{1,0:T(2,128)}, u32[]{:S(2)}) copy-start(f32[2,768]{1,0:T(2,128)} %get-tuple-element.106) | copy-start | bytes 18436
  160.1 9.0 %copy-start.50 = (f32[768]{0:T(1024)S(1)}, f32[768]{0:T(1024)}, u32[]{:S(2)}) copy-start(f32[768]{0:T(1024)} %get-tuple-element.87) | copy-start | bytes 9220
  160.1 14.1 %collective-permute-start.3 = (bf16[2,64,768]{2,1,0:T(8,128)(2,1)}, bf16[2,64,768]{2,1,0:T(8,128)(2,1)S(1)}, u32[]{:S(2)}, u32[]{:S(2)}) collective-permute-start(bf16[2,64,768]{2,1,0:T(8,128)(2,1)} %get-tuple-element.36), channel_id=1, source_target_pairs={{0,1},{1,2},{2,3},{3,0},{4,5},{5,6},{6,7},{7,4},{8,9},{9,10},{10,1... | collective-permute-start | bytes 589832 | tf_op jit(solution)/shard_map/ppermute | solution.py:148
  163.5 14.7 %collective-permute-start.4 = (bf16[2,64,768]{2,1,0:T(8,128)(2,1)}, bf16[2,64,768]{2,1,0:T(8,128)(2,1)}, u32[]{:S(2)}, u32[]{:S(2)}) collective-permute-start(bf16[2,64,768]{2,1,0:T(8,128)(2,1)} %get-tuple-element.36), channel_id=1, source_target_pairs={{0,2},{1,3},{2,0},{3,1},{4,6},{5,7},{6,4},{7,5},{8,10},{9,11},{10,... | collective-permute-start | bytes 589832 | tf_op jit(solution)/shard_map/ppermute | solution.py:148
  166.3 20.1 %collective-permute-start.5 = (bf16[2,64,768]{2,1,0:T(8,128)(2,1)}, bf16[2,64,768]{2,1,0:T(8,128)(2,1)}, u32[]{:S(2)}, u32[]{:S(2)}) collective-permute-start(bf16[2,64,768]{2,1,0:T(8,128)(2,1)} %get-tuple-element.36), channel_id=1, source_target_pairs={{0,3},{1,0},{2,1},{3,2},{4,7},{5,4},{6,5},{7,6},{8,11},{9,8},{10,9... | collective-permute-start | bytes 589832 | tf_op jit(solution)/shard_map/ppermute | solution.py:148
  212.9 27.4 %copy-start.57 = (f32[3,64]{1,0:T(4,128)S(1)}, f32[3,64]{1,0:T(4,128)}, u32[]{:S(2)}) copy-start(f32[3,64]{1,0:T(4,128)} %get-tuple-element.108) | copy-start | bytes 2308
  212.9 27.5 %copy-start.64 = (f32[1,192]{1,0:T(1,128)S(1)}, f32[1,192]{1,0:T(1,128)}, u32[]{:S(2)}) copy-start(f32[1,192]{1,0:T(1,128)} %stack.43) | copy-start | bytes 2308
  213.0 27.6 %copy-start.42 = (f32[4992]{0:T(1024)S(1)}, f32[4992]{0:T(1024)}, u32[]{:S(2)}) copy-start(f32[4992]{0:T(1024)} %custom-call) | copy-start | bytes 59908
  214.8 25.8 %copy-start.63 = (f32[768]{0:T(1024)S(1)}, f32[768]{0:T(1024)}, u32[]{:S(2)}) copy-start(f32[768]{0:T(1024)} %get-tuple-element.125) | copy-start | bytes 9220
  214.8 25.8 %copy-start.51 = (f32[768]{0:T(1024)S(1)}, f32[768]{0:T(1024)}, u32[]{:S(2)}) copy-start(f32[768]{0:T(1024)} %fusion.18) | copy-start | bytes 9220
  214.8 38.0 %slice-start = ((f32[96,768]{1,0:T(8,128)}), f32[96,576]{1,0:T(8,128)S(1)}, s32[]{:S(2)}) async-start(f32[96,768]{1,0:T(8,128)} %copy-done.15), calls=%async_computation | async-start | bytes 491520 | tf_op jit(solution)/shard_map/slice | solution.py:324
  240.3 17.2 %copy-start.31 = (bf16[2,768]{1,0:T(2,128)(2,1)S(1)}, bf16[2,768]{1,0:T(2,128)(2,1)}, u32[]{:S(2)}) copy-start(bf16[2,768]{1,0:T(2,128)(2,1)} %param.15) | copy-start | bytes 9220
  240.3 17.8 %copy-start.21 = (bf16[2,256,768]{2,1,0:T(8,128)(2,1)S(1)}, bf16[2,256,768]{2,1,0:T(8,128)(2,1)}, u32[]{:S(2)}) copy-start(bf16[2,256,768]{2,1,0:T(8,128)(2,1)} %get-tuple-element.45) | copy-start | bytes 2359300
  254.5 6.7 %copy-start.19 = (bf16[2,256,768]{2,1,0:T(8,128)(2,1)S(1)}, bf16[2,256,768]{2,1,0:T(8,128)(2,1)}, u32[]{:S(2)}) copy-start(bf16[2,256,768]{2,1,0:T(8,128)(2,1)} %copy-done.18) | copy-start | bytes 2359300
  (47 other events, 116.1 us)

commit v3 on v2

--- a/solution.py
+++ b/solution.py
@@ -329,30 +329,25 @@
     dscale_one = jnp.sum(dh_one * norm_one_own, axis=1)
     dshift_one = jnp.sum(dh_one, axis=1)
     grad_own = dx_one + norm_back(dh_one * (1.0 + scale_one), norm_one_own, recip_one_own)
-    stats_own = jnp.concatenate(
-        [
-            jnp.stack(
-                [dshift_one, dscale_one, dgate_one, dshift_two, dscale_two, dgate_two], axis=1
-            ).reshape(lat_cap * 6, width),
-            grad_proj_part[None],
-        ],
-        axis=0,
-    )
-    grad_gathered, stats_all = exchange(
-        7, ("tensor", "gather_rows", to_half(grad_own)), ("tensor", "gather", stats_own)
+    stats_own = jnp.stack(
+        [dshift_one, dscale_one, dgate_one, dshift_two, dscale_two, dgate_two], axis=1
+    ).reshape(lat_cap, tensor_count, local_cols)
+    stats_own = jnp.swapaxes(stats_own, 0, 1)
+    grad_gathered, stats_arrived, proj_all = exchange(
+        7,
+        ("tensor", "gather_rows", to_half(grad_own)),
+        ("tensor", "scatter", stats_own),
+        ("tensor", "gather", grad_proj_part[None]),
     )
     grad_latents = grad_gathered.astype(jnp.float32)
-    stats_sum = jnp.sum(stats_all, axis=0)
-    dmod = stats_sum[: lat_cap * 6].reshape(lat_cap, 6 * width)
-    col_start = tensor_index * local_cols
-    dmod_local = lax.dynamic_slice_in_dim(dmod, col_start, local_cols, 1)
+    dmod_local = sum_blocks(stats_own, stats_arrived, tensor_index)
     cond_part = contract_lowprec("le,de->ld", to_half(dmod_local), ada_weight)
     vectors = [
         dmod_local.reshape(-1),
         grad_qv.reshape(-1),
         grad_fc1_b,
         grad_fc2_part,
-        stats_sum[lat_cap * 6],
+        jnp.sum(proj_all[:, 0], axis=0),
     ]
     packed_all, cond_all = exchange(
         8, ("dp", "gather", jnp.concatenate(vectors)[None]), ("tensor", "gather", cond_part)

time: 265 us -> 258 us (0.974)
  Pallas kernels: 138 us -> 135 us
  waiting for transfers between devices: 2.43 us -> 5.34 us
  local copies, waits for them, and re-layouts: 30.4 us -> 27.6 us
  other arithmetic: 40.9 us -> 38.2 us
    pallas_call x8, Pallas kernels: 138 us -> 135 us  [exchange(): pl.pallas_call(functools.partial(exchange_body, kinds, sizes, copy_count)...]
    ppermute x6, waiting for transfers between devices: 2.43 us -> 5.34 us  [shift_tensor(): lax.ppermute(array, 'tensor', [(i, (i + step) % size) for i in range(size)])]
    reduce_sum x3 -> x4, other arithmetic: 4.96 us -> 5.73 us  [sum_blocks(): return own + jnp.sum(arrived.astype(jnp.float32), axis=0)]
    unnamed x151 -> x149, local copies, waits for them, and re-layouts: 7.81 us -> 8.29 us
  transfers between devices with their start and end apart: 6 -> 6, of which waited for: 1 -> 1; matrix products, arithmetic and copies ran while one was open for 15% -> 15% of each run, Pallas kernels for 6% -> 7%
where the time goes in v3:
time: 258 us; the launch traced here: 257 us
  Pallas kernels  135 us (52%)
  other arithmetic  38.2 us (15%)
  matrix products  36.3 us (14%)
  local copies, waits for them, and re-layouts  27.6 us (11%)
  starting transfers between devices  12.1 us (5%)
  waiting for transfers between devices  5.34 us (2%)
    pallas_call x8, Pallas kernels, exchange(): pl.pallas_call(functools.partial(exchange_body, kinds, sizes, copy_count)...  135 us
    dot_general x19, matrix products, contract_lowprec(): return jnp.einsum(form, left, right, preferred_element_type=jnp.float32)  31.5 us
    ppermute x6, starting transfers between devices, shift_tensor(): lax.ppermute(array, 'tensor', [(i, (i + step) % size) for i in range(size)])  12.1 us
    unnamed x149, local copies, waits for them, and re-layouts  8.29 us
    reduce_sum x4, other arithmetic, sum_blocks(): return own + jnp.sum(arrived.astype(jnp.float32), axis=0)  5.73 us
    ppermute x6, waiting for transfers between devices, shift_tensor(): lax.ppermute(array, 'tensor', [(i, (i + step) % size) for i in range(size)])  5.34 us
  transfers between devices with their start and end apart: 6, of which 1 were waited for; matrix products, arithmetic and copies ran while one was open for 15% of the time, Pallas kernels for 7%

profile of v3, /device:TPU:0, one launch (start us, length us, event | category | flops | bytes accessed | tf_op | source)
XLA Modules:
  0.0 256.6 jit_solution(18080693618263062808)
XLA Ops:
  3.9 9.7 %shard_map.237 = (f32[4,2,1152]{2,1,0:T(2,128)}, f32[8,2,768]{2,1,0:T(2,128)}) custom-call(f32[2,1152]{1,0:T(2,128)} %convolution_add_fusion.refs_0_, f32[2,768]{1,0:T(2,128)} %fusion.58.refs_1_), custom_call_target="tpu_custom_call" | custom-call | tf_op jit(solution)/shard_map/pallas_call | solution.py:132
  27.1 17.5 %shard_map.238 = bf16[3,2,64,768]{3,2,1,0:T(8,128)(2,1)} custom-call(bf16[2,256,768]{2,1,0:T(8,128)(2,1)} %convolution_convert_fusion.2.refs_0_), custom_call_target="tpu_custom_call" | custom-call | tf_op jit(solution)/shard_map/pallas_call | solution.py:132
  44.6 1.9 convert_reduce_fusion.5
  49.5 19.3 %shard_map.239 = bf16[2,256,768]{2,1,0:T(8,128)(2,1)} custom-call(bf16[2,64,768]{2,1,0:T(8,128)(2,1)} %add_convert_fusion.2.refs_0_), custom_call_target="tpu_custom_call" | custom-call | tf_op jit(solution)/shard_map/pallas_call | solution.py:132
  68.9 2.4 convolution_add_fusion.1
  72.4 2.0 convolution_convert_fusion.1
  74.4 1.9 constant_dynamic-slice_fusion.5
  76.3 3.7 %collective-permute-start = (bf16[2,64,768]{2,1,0:T(8,128)(2,1)}, bf16[2,64,768]{2,1,0:T(8,128)(2,1)}, u32[]{:S(2)}, u32[]{:S(2)}) collective-permute-start(bf16[2,64,768]{2,1,0:T(8,128)(2,1)} %get-tuple-element.102), channel_id=1, source_target_pairs={{0,1},{1,2},{2,3},{3,0},{4,5},{5,6},{6,7},{7,4},{8,9},{9,10},{10,1... | collective-permute-start | bytes 589832 | tf_op jit(solution)/shard_map/ppermute | solution.py:148
  80.0 2.1 collective-permute-start.1
  83.1 4.2 %fusion.69 = (f32[768]{0:T(1024)}, bf16[2,256,768]{2,1,0:T(8,128)(2,1)S(1)}) fusion(f32[2,256,768]{2,1,0:T(8,128)} %copy-done.67, bf16[768,768]{1,0:T(8,128)(2,1)} %param.25, bf16[2,256,768]{2,1,0:T(8,128)(2,1)} %param.27, f32[2]{0:T(128)S(1)} %compare_convert_fusion, f32[2,768]{1,0:T(2,128)} %get-tuple-element.116), kind=kOutput, calls=%fused_computation.171 | convolution fusion | flops 613416192 | bytes 4334600 | tf_op jit(solution)/shard_map/vug,bg->vub/dot_general | solution.py:49
  87.3 1.9 bitcast_convert_fusion.1
  90.9 2.1 bitcast_convert_fusion
  94.5 17.0 %shard_map.240 = (bf16[3,2,64,768]{3,2,1,0:T(8,128)(2,1)}, bf16[7,96,768]{2,1,0:T(8,128)(2,1)}) custom-call(bf16[2,256,768]{2,1,0:T(8,128)(2,1)} %convolution_convert_fusion.refs_0_, bf16[8,96,768]{2,1,0:T(8,128)(2,1)} %bitcast.152), custom_call_target="tpu_custom_call" | custom-call | tf_op jit(solution)/shard_map/pallas_call | solution.py:132
  111.5 1.9 convert_reduce_fusion.4
  113.4 2.1 convert_reduce_fusion.1
  121.4 2.1 fusion.18
  123.5 3.4 %multiply_reduce_fusion.2 = (f32[2,768]{1,0:T(2,128)}, bf16[2,64,768]{2,1,0:T(8,128)(2,1)}, f32[2,768]{1,0:T(2,128)}, f32[2,64]{1,0:T(2,128)S(1)}, f32[2,64]{1,0...) fusion(f32[2]{0:T(128)} %copy-done.59, bf16[2,256,768]{2,1,0:T(8,128)(2,1)} %param.27, s32[]{:T(128)S(6)} %select_n.49, ...), kind=kLoop, calls=%fused_computation.69 | loop fusion | flops 2649344 | bytes 2591756 | tf_op jit(solution)/shard_map/reduce_sum | solution.py:287
  127.0 1.9 multiply_reduce_fusion.9
  130.4 21.7 %shard_map.241 = (bf16[2,256,768]{2,1,0:T(8,128)(2,1)}, bf16[7,96,768]{2,1,0:T(8,128)(2,1)}) custom-call(bf16[2,64,768]{2,1,0:T(8,128)(2,1)} %multiply_convert_fusion.2.refs_0_, bf16[8,96,768]{2,1,0:T(8,128)(2,1)} %bitcast.150), custom_call_target="tpu_custom_call" | custom-call | tf_op jit(solution)/shard_map/pallas_call | solution.py:132
  152.1 2.3 convolution_convert_fusion.4
  154.4 3.1 %multiply_convert_fusion = bf16[2,3,256,256]{2,3,1,0:T(8,128)(2,1)} fusion(f32[2,3,256,256]{2,3,1,0:T(8,128)S(1)} %get-tuple-element.124, f32[2,3,256]{2,1,0:T(4,128)S(1)} %copy-done.29, bf16[2,256,3,64]{1,3,2,0:T(8,128)(2,1)} %bitcast.156, f32[2,256,3,64]{1,3,2,0:T(8,128)} %bitcast.149, f32[3,64]{1,0:T(4,128)S(1)} %copy-done.56), kind=kOutput, calls=%fused_computation.26 | convolution fusion | flops 103810816 | bytes 2956032 | tf_op jit(solution)/shard_map/sub | solution.py:299
  157.5 2.1 fusion.66
  159.5 3.3 %collective-permute-start.3 = (bf16[2,64,768]{2,1,0:T(8,128)(2,1)}, bf16[2,64,768]{2,1,0:T(8,128)(2,1)S(1)}, u32[]{:S(2)}, u32[]{:S(2)}) collective-permute-start(bf16[2,64,768]{2,1,0:T(8,128)(2,1)} %get-tuple-element.37), channel_id=1, source_target_pairs={{0,1},{1,2},{2,3},{3,0},{4,5},{5,6},{6,7},{7,4},{8,9},{9,10},{10,1... | collective-permute-start | bytes 589832 | tf_op jit(solution)/shard_map/ppermute | solution.py:148
  162.8 2.5 collective-permute-start.4
  169.3 1.9 fusion.34
  172.1 5.3 %collective-permute-done.4 = bf16[2,64,768]{2,1,0:T(8,128)(2,1)} collective-permute-done((bf16[2,64,768]{2,1,0:T(8,128)(2,1)}, bf16[2,64,768]{2,1,0:T(8,128)(2,1)}, u32[]{:S(2)}, u32[]{:S(2)}) %collective-permute-start.4) | collective-permute-done | bytes 196640 | tf_op jit(solution)/shard_map/ppermute | solution.py:148
  178.4 2.2 concatenate.11
  180.6 2.1 copy.46
  182.7 3.0 %bitcast_convert_fusion.3.refs_0_ = bf16[2,256,768]{2,1,0:T(8,128)(2,1)} fusion(bf16[2,256,3,192]{1,3,0,2:T(8,128)(2,1)} %copy-done.24, bf16[768,3,192]{0,2,1:T(8,128)(2,1)} %param.19), kind=kOutput, calls=%fused_computation.25 | convolution fusion | flops 453378048 | bytes 2260992 | tf_op jit(solution)/shard_map/lsce,dce->lsd/dot_general | solution.py:49
  187.0 20.0 %shard_map.242 = (bf16[3,2,64,768]{3,2,1,0:T(8,128)(2,1)}, bf16[7,96,768]{2,1,0:T(8,128)(2,1)}) custom-call(bf16[2,256,768]{2,1,0:T(8,128)(2,1)} %bitcast_convert_fusion.3.refs_0_, bf16[8,96,768]{2,1,0:T(8,128)(2,1)} %pad_maximum_fusion.refs_1_), custom_call_target="tpu_custom_call" | custom-call | tf_op jit(solution)/shard_map/pallas_call | solution.py:132
  212.3 21.0 %shard_map.243 = (bf16[2,256,768]{2,1,0:T(8,128)(2,1)}, f32[3,2,1152]{2,1,0:T(2,128)}, f32[4,1,768]{2,1,0:T(1,128)}) custom-call(bf16[2,64,768]{2,1,0:T(8,128)(2,1)} %add_convert_fusion.1.refs_0_, f32[4,2,1152]{2,1,0:T(2,128)} %bitcast.162, f32[1,768]{1,0:T(1,128)} %broadcast_in_dim.10.refs_2_), custom_call_target="tpu_custom_call" | custom-call | tf_op jit(solution)/shard_map/pallas_call | solution.py:132
  236.9 8.5 %shard_map.244 = (f32[8,1,4992]{2,1,0:T(1,128)}, f32[4,2,768]{2,1,0:T(2,128)}) custom-call(f32[1,4992]{1,0:T(1,128)} %broadcast_in_dim.11.refs_0_, f32[2,768]{1,0:T(2,128)} %fusion.56.refs_1_), custom_call_target="tpu_custom_call" | custom-call | tf_op jit(solution)/shard_map/pallas_call | solution.py:132
  (241 shorter events, 58.0 us)
Async XLA Ops:
  0.7 14.3 %copy-start.1 = (bf16[2,256,768]{2,1,0:T(8,128)(2,1)S(1)}, bf16[2,256,768]{2,1,0:T(8,128)(2,1)}, u32[]{:S(2)}) copy-start(bf16[2,256,768]{2,1,0:T(8,128)(2,1)} %param.14) | copy-start | bytes 2359300
  2.1 13.4 %copy-start.66 = (bf16[768,3,192]{0,2,1:T(8,128)(2,1)S(1)}, bf16[768,3,192]{0,2,1:T(8,128)(2,1)}, u32[]{:S(2)}) copy-start(bf16[768,3,192]{0,2,1:T(8,128)(2,1)} %param.19) | copy-start | bytes 2654212
  76.3 47.2 %collective-permute-start = (bf16[2,64,768]{2,1,0:T(8,128)(2,1)}, bf16[2,64,768]{2,1,0:T(8,128)(2,1)}, u32[]{:S(2)}, u32[]{:S(2)}) collective-permute-start(bf16[2,64,768]{2,1,0:T(8,128)(2,1)} %get-tuple-element.102), channel_id=1, source_target_pairs={{0,1},{1,2},{2,3},{3,0},{4,5},{5,6},{6,7},{7,4},{8,9},{9,10},{10,1... | collective-permute-start | bytes 589832 | tf_op jit(solution)/shard_map/ppermute | solution.py:148
  80.0 43.5 %collective-permute-start.1 = (bf16[2,64,768]{2,1,0:T(8,128)(2,1)}, bf16[2,64,768]{2,1,0:T(8,128)(2,1)}, u32[]{:S(2)}, u32[]{:S(2)}) collective-permute-start(bf16[2,64,768]{2,1,0:T(8,128)(2,1)} %get-tuple-element.104), channel_id=1, source_target_pairs={{0,2},{1,3},{2,0},{3,1},{4,6},{5,7},{6,4},{7,5},{8,10},{9,11},{10,... | collective-permute-start | bytes 589832 | tf_op jit(solution)/shard_map/ppermute | solution.py:148
  82.2 41.3 %collective-permute-start.2 = (bf16[2,64,768]{2,1,0:T(8,128)(2,1)}, bf16[2,64,768]{2,1,0:T(8,128)(2,1)}, u32[]{:S(2)}, u32[]{:S(2)}) collective-permute-start(bf16[2,64,768]{2,1,0:T(8,128)(2,1)} %get-tuple-element.103), channel_id=1, source_target_pairs={{0,3},{1,0},{2,1},{3,2},{4,7},{5,4},{6,5},{7,6},{8,11},{9,8},{10,9... | collective-permute-start | bytes 589832 | tf_op jit(solution)/shard_map/ppermute | solution.py:148
  83.1 7.8 %copy-start.59 = (f32[2]{0:T(128)}, f32[2]{0:T(128)S(1)}, u32[]{:S(2)}) copy-start(f32[2]{0:T(128)S(1)} %compare_convert_fusion) | copy-start | bytes 28
  121.3 5.6 %copy-start.5 = (f32[2,64,768]{2,1,0:T(8,128)S(1)}, f32[2,64,768]{2,1,0:T(8,128)}, u32[]{:S(2)}) copy-start(f32[2,64,768]{2,1,0:T(8,128)} %copy-done.4) | copy-start | bytes 1179652
  121.3 5.6 %copy-start.10 = (f32[2,64,768]{2,1,0:T(8,128)S(1)}, f32[2,64,768]{2,1,0:T(8,128)}, u32[]{:S(2)}) copy-start(f32[2,64,768]{2,1,0:T(8,128)} %convert_reduce_fusion.5) | copy-start | bytes 1179652
  121.3 5.6 %copy-start.35 = (f32[2,64]{1,0:T(2,128)S(1)}, f32[2,64]{1,0:T(2,128)}, u32[]{:S(2)}) copy-start(f32[2,64]{1,0:T(2,128)} %copy-done.34) | copy-start | bytes 1540
  121.4 5.6 %copy-start.47 = (f32[768]{0:T(1024)S(1)}, f32[768]{0:T(1024)}, u32[]{:S(2)}) copy-start(f32[768]{0:T(1024)} %param.22) | copy-start | bytes 9220
  121.4 5.6 %copy-start.49 = (f32[2,64]{1,0:T(2,128)S(1)}, f32[2,64]{1,0:T(2,128)}, u32[]{:S(2)}) copy-start(f32[2,64]{1,0:T(2,128)} %copy-done.48) | copy-start | bytes 1540
  121.4 5.6 %copy-start.60 = (f32[2]{0:T(128)S(1)}, f32[2]{0:T(128)}, u32[]{:S(2)}) copy-start(f32[2]{0:T(128)} %copy-done.59) | copy-start | bytes 28
  129.7 24.7 %copy-start.29 = (f32[2,3,256]{2,1,0:T(4,128)S(1)}, f32[2,3,256]{2,1,0:T(4,128)}, u32[]{:S(2)}) copy-start(f32[2,3,256]{2,1,0:T(4,128)} %log_add_fusion) | copy-start | bytes 18436
  130.4 24.0 %copy-start.56 = (f32[3,64]{1,0:T(4,128)S(1)}, f32[3,64]{1,0:T(4,128)}, u32[]{:S(2)}) copy-start(f32[3,64]{1,0:T(4,128)} %add.275) | copy-start | bytes 2308
  157.5 7.8 %copy-start.11 = (bf16[2,256,768]{2,1,0:T(8,128)(2,1)S(1)}, bf16[2,256,768]{2,1,0:T(8,128)(2,1)}, u32[]{:S(2)}) copy-start(bf16[2,256,768]{2,1,0:T(8,128)(2,1)} %get-tuple-element.38) | copy-start | bytes 2359300
  157.5 7.8 %copy-start.14 = (bf16[2,3,64,256]{3,2,1,0:T(8,128)(2,1)S(1)}, bf16[2,3,64,256]{3,2,1,0:T(8,128)(2,1)}, u32[]{:S(2)}) copy-start(bf16[2,3,64,256]{3,2,1,0:T(8,128)(2,1)} %copy-done.13) | copy-start | bytes 589828
  157.5 8.6 %copy-start.50 = (f32[768]{0:T(1024)S(1)}, f32[768]{0:T(1024)}, u32[]{:S(2)}) copy-start(f32[768]{0:T(1024)} %get-tuple-element.87) | copy-start | bytes 9220
  159.5 11.7 %collective-permute-start.3 = (bf16[2,64,768]{2,1,0:T(8,128)(2,1)}, bf16[2,64,768]{2,1,0:T(8,128)(2,1)S(1)}, u32[]{:S(2)}, u32[]{:S(2)}) collective-permute-start(bf16[2,64,768]{2,1,0:T(8,128)(2,1)} %get-tuple-element.37), channel_id=1, source_target_pairs={{0,1},{1,2},{2,3},{3,0},{4,5},{5,6},{6,7},{7,4},{8,9},{9,10},{10,1... | collective-permute-start | bytes 589832 | tf_op jit(solution)/shard_map/ppermute | solution.py:148
  162.8 14.6 %collective-permute-start.4 = (bf16[2,64,768]{2,1,0:T(8,128)(2,1)}, bf16[2,64,768]{2,1,0:T(8,128)(2,1)}, u32[]{:S(2)}, u32[]{:S(2)}) collective-permute-start(bf16[2,64,768]{2,1,0:T(8,128)(2,1)} %get-tuple-element.37), channel_id=1, source_target_pairs={{0,2},{1,3},{2,0},{3,1},{4,6},{5,7},{6,4},{7,5},{8,10},{9,11},{10,... | collective-permute-start | bytes 589832 | tf_op jit(solution)/shard_map/ppermute | solution.py:148
  165.6 20.1 %collective-permute-start.5 = (bf16[2,64,768]{2,1,0:T(8,128)(2,1)}, bf16[2,64,768]{2,1,0:T(8,128)(2,1)}, u32[]{:S(2)}, u32[]{:S(2)}) collective-permute-start(bf16[2,64,768]{2,1,0:T(8,128)(2,1)} %get-tuple-element.37), channel_id=1, source_target_pairs={{0,3},{1,0},{2,1},{3,2},{4,7},{5,4},{6,5},{7,6},{8,11},{9,8},{10,9... | collective-permute-start | bytes 589832 | tf_op jit(solution)/shard_map/ppermute | solution.py:148
  171.2 6.2 %copy-start.3 = (bf16[2,256,768]{2,1,0:T(8,128)(2,1)S(1)}, bf16[2,256,768]{2,1,0:T(8,128)(2,1)}, u32[]{:S(2)}) copy-start(bf16[2,256,768]{2,1,0:T(8,128)(2,1)} %param.14) | copy-start | bytes 2359300
  171.2 6.2 %copy-start.31 = (f32[2,768]{1,0:T(2,128)S(1)}, f32[2,768]{1,0:T(2,128)}, u32[]{:S(2)}) copy-start(f32[2,768]{1,0:T(2,128)} %copy-done.30) | copy-start | bytes 18436
  171.2 6.2 %copy-start.45 = (f32[2,256]{1,0:T(2,128)S(1)}, f32[2,256]{1,0:T(2,128)}, u32[]{:S(2)}) copy-start(f32[2,256]{1,0:T(2,128)} %copy-done.43) | copy-start | bytes 6148
  171.2 6.2 %copy-start.54 = (f32[2,256]{1,0:T(2,128)S(1)}, f32[2,256]{1,0:T(2,128)}, u32[]{:S(2)}) copy-start(f32[2,256]{1,0:T(2,128)} %copy-done.52) | copy-start | bytes 6148
  171.3 6.2 %copy-start.58 = (f32[2,768]{1,0:T(2,128)S(1)}, f32[2,768]{1,0:T(2,128)}, u32[]{:S(2)}) copy-start(f32[2,768]{1,0:T(2,128)} %copy-done.57) | copy-start | bytes 18436
  172.1 5.3 %copy-start.24 = (bf16[2,256,3,192]{1,3,0,2:T(8,128)(2,1)}, bf16[2,256,3,192]{1,3,0,2:T(8,128)(2,1)S(1)}, u32[]{:S(2)}) copy-start(bf16[2,256,3,192]{1,3,0,2:T(8,128)(2,1)S(1)} %pad_maximum_fusion.1) | copy-start | bytes 1769476
  211.4 24.8 %copy-start.42 = (f32[4992]{0:T(1024)S(1)}, f32[4992]{0:T(1024)}, u32[]{:S(2)}) copy-start(f32[4992]{0:T(1024)} %custom-call) | copy-start | bytes 59908
  211.4 24.8 %copy-start.61 = (f32[768]{0:T(1024)S(1)}, f32[768]{0:T(1024)}, u32[]{:S(2)}) copy-start(f32[768]{0:T(1024)} %get-tuple-element.127) | copy-start | bytes 9220
  211.4 24.8 %copy-start.51 = (f32[768]{0:T(1024)S(1)}, f32[768]{0:T(1024)}, u32[]{:S(2)}) copy-start(f32[768]{0:T(1024)} %fusion.18) | copy-start | bytes 9220
  212.3 34.8 %slice-start = ((f32[96,768]{1,0:T(8,128)}), f32[96,576]{1,0:T(8,128)S(1)}, s32[]{:S(2)}) async-start(f32[96,768]{1,0:T(8,128)} %copy-done.16), calls=%async_computation | async-start | bytes 491520 | tf_op jit(solution)/shard_map/slice | solution.py:324
  235.9 14.2 %copy-start.33 = (bf16[2,768]{1,0:T(2,128)(2,1)S(1)}, bf16[2,768]{1,0:T(2,128)(2,1)}, u32[]{:S(2)}) copy-start(bf16[2,768]{1,0:T(2,128)(2,1)} %param.15) | copy-start | bytes 9220
  235.9 14.8 %copy-start.22 = (bf16[2,256,768]{2,1,0:T(8,128)(2,1)S(1)}, bf16[2,256,768]{2,1,0:T(8,128)(2,1)}, u32[]{:S(2)}) copy-start(bf16[2,256,768]{2,1,0:T(8,128)(2,1)} %get-tuple-element.46) | copy-start | bytes 2359300
  (44 other events, 97.8 us)

commit v4 on v3

--- a/solution.py
+++ b/solution.py
@@ -308,21 +308,24 @@
         lat_cap, seq_len, local_width
     )
     grad_qv = jnp.stack([jnp.sum(dquery, axis=(0, 1)), jnp.sum(dvalue, axis=(0, 1))], axis=0)
-    dqkv_b = to_half(jnp.stack([dquery, dkey, dvalue], axis=2))
+    dqkv_b = to_half(jnp.concatenate([dquery, dkey, dvalue], axis=2))
     parts[2 % tensor_count], dqkv_b = lax.optimization_barrier((parts[2 % tensor_count], dqkv_b))
-    grad_qkv = contract_lowprec("lsd,lsce->dce", h_one, dqkv_b)
-    dh_part_one = to_half(contract_lowprec("lsce,dce->lsd", dqkv_b, qkv_weight))
+    grad_qkv = contract_lowprec("lsd,lsf->df", h_one, dqkv_b)
+    dh_part_one = to_half(contract_lowprec(
+        "lsf,df->lsd", dqkv_b, qkv_weight.reshape(width, 3 * local_width)
+    ))
     parts[3 % tensor_count], dh_part_one = lax.optimization_barrier((parts[3 % tensor_count], dh_part_one))
     block_output = place_rows(parts)
-    attn_gradient = jnp.concatenate(
-        [to_half(grad_qkv).reshape(width, 3 * local_width), to_half(grad_proj)], axis=1
-    ).reshape(dp_count, width // dp_count, 4 * local_width)
-    dh_arrived, attn_gradient_arrived = exchange(
-        6, ("tensor", "scatter_rows", dh_part_one), ("dp", "scatter", attn_gradient)
-    )
-    summed_attn = sum_blocks(attn_gradient, attn_gradient_arrived, dp_index)
-    summed_qkv = summed_attn[:, : 3 * local_width].reshape(-1, 3, local_width)
-    summed_proj = summed_attn[:, 3 * local_width :].T
+    qkv_blocks = to_half(grad_qkv).reshape(dp_count, width // dp_count, 3 * local_width)
+    proj_blocks = to_half(grad_proj).reshape(dp_count, width // dp_count, local_width)
+    dh_arrived, qkv_arrived, proj_arrived = exchange(
+        6,
+        ("tensor", "scatter_rows", dh_part_one),
+        ("dp", "scatter", qkv_blocks),
+        ("dp", "scatter", proj_blocks),
+    )
+    summed_qkv = sum_blocks(qkv_blocks, qkv_arrived, dp_index).reshape(-1, 3, local_width)
+    summed_proj = sum_blocks(proj_blocks, proj_arrived, dp_index).T
     dh_one = sum_rows(dh_part_one, dh_arrived, row_start)
     norm_one_own = lax.dynamic_slice_in_dim(norm_one, row_start, rows_dev, 1)
     recip_one_own = lax.dynamic_slice_in_dim(recip_one, row_start, rows_dev, 1)

time: 258 us -> 257 us (level)
  local copies, waits for them, and re-layouts: 27.6 us -> 24.3 us
    concatenate x2 -> x0, local copies, waits for them, and re-layouts: 4.34 us -> none  [per_device(): jnp.concatenate([to_half(grad_qkv).reshape(width, 3 * local_width), to_ha...]
    reduce_sum x4 -> x5, other arithmetic: 5.73 us -> 3.18 us  [sum_blocks(): return own + jnp.sum(arrived.astype(jnp.float32), axis=0)]
    unnamed x149 -> x151, local copies, waits for them, and re-layouts: 8.29 us -> 6.99 us
  transfers between devices with their start and end apart: 6 -> 6, of which waited for: 1 -> 2; matrix products, arithmetic and copies ran while one was open for 15% -> 14% of each run, Pallas kernels for 7% -> 7%
where the time goes in v4:
time: 257 us; the launch traced here: 256 us
  Pallas kernels  136 us (53%)
  other arithmetic  37.8 us (15%)
  matrix products  37.4 us (15%)
  local copies, waits for them, and re-layouts  24.3 us (9%)
  starting transfers between devices  11.9 us (5%)
  waiting for transfers between devices  6.21 us (2%)
    pallas_call x8, Pallas kernels, exchange(): pl.pallas_call(functools.partial(exchange_body, kinds, sizes, copy_count)...  136 us
    dot_general x19, matrix products, contract_lowprec(): return jnp.einsum(form, left, right, preferred_element_type=jnp.float32)  32.6 us
    ppermute x6, starting transfers between devices, shift_tensor(): lax.ppermute(array, 'tensor', [(i, (i + step) % size) for i in range(size)])  11.9 us
    unnamed x151, local copies, waits for them, and re-layouts  6.99 us
    ppermute x6, waiting for transfers between devices, shift_tensor(): lax.ppermute(array, 'tensor', [(i, (i + step) % size) for i in range(size)])  6.21 us
  transfers between devices with their start and end apart: 6, of which 2 were waited for; matrix products, arithmetic and copies ran while one was open for 14% of the time, Pallas kernels for 7%

profile of v4, /device:TPU:0, one launch (start us, length us, event | category | flops | bytes accessed | tf_op | source)
XLA Modules:
  0.0 255.8 jit_solution(17985824440914811408)
XLA Ops:
  3.9 9.7 %shard_map.237 = (f32[4,2,1152]{2,1,0:T(2,128)}, f32[8,2,768]{2,1,0:T(2,128)}) custom-call(f32[2,1152]{1,0:T(2,128)} %convolution_add_fusion.refs_0_, f32[2,768]{1,0:T(2,128)} %fusion.56.refs_1_), custom_call_target="tpu_custom_call" | custom-call | tf_op jit(solution)/shard_map/pallas_call | solution.py:132
  27.1 17.5 %shard_map.238 = bf16[3,2,64,768]{3,2,1,0:T(8,128)(2,1)} custom-call(bf16[2,256,768]{2,1,0:T(8,128)(2,1)} %convolution_convert_fusion.3.refs_0_), custom_call_target="tpu_custom_call" | custom-call | tf_op jit(solution)/shard_map/pallas_call | solution.py:132
  44.6 1.9 convert_reduce_fusion.5
  49.5 19.3 %shard_map.239 = bf16[2,256,768]{2,1,0:T(8,128)(2,1)} custom-call(bf16[2,64,768]{2,1,0:T(8,128)(2,1)} %add_convert_fusion.2.refs_0_), custom_call_target="tpu_custom_call" | custom-call | tf_op jit(solution)/shard_map/pallas_call | solution.py:132
  68.9 2.4 convolution_add_fusion.1
  72.4 2.0 convolution_convert_fusion.1
  74.4 1.9 constant_dynamic-slice_fusion.5
  76.3 3.7 %collective-permute-start = (bf16[2,64,768]{2,1,0:T(8,128)(2,1)}, bf16[2,64,768]{2,1,0:T(8,128)(2,1)}, u32[]{:S(2)}, u32[]{:S(2)}) collective-permute-start(bf16[2,64,768]{2,1,0:T(8,128)(2,1)} %get-tuple-element.117), channel_id=1, source_target_pairs={{0,1},{1,2},{2,3},{3,0},{4,5},{5,6},{6,7},{7,4},{8,9},{9,10},{10,1... | collective-permute-start | bytes 589832 | tf_op jit(solution)/shard_map/ppermute | solution.py:148
  80.0 2.1 collective-permute-start.1
  83.1 4.2 %fusion.67 = (f32[768]{0:T(1024)}, bf16[2,256,768]{2,1,0:T(8,128)(2,1)S(1)}) fusion(f32[2,256,768]{2,1,0:T(8,128)} %copy-done.68, bf16[768,768]{1,0:T(8,128)(2,1)} %param.25, bf16[2,256,768]{2,1,0:T(8,128)(2,1)} %param.27, f32[2]{0:T(128)S(1)} %compare_convert_fusion, f32[2,768]{1,0:T(2,128)} %get-tuple-element.131), kind=kOutput, calls=%fused_computation.167 | convolution fusion | flops 613416192 | bytes 4334600 | tf_op jit(solution)/shard_map/vug,bg->vub/dot_general | solution.py:49
  87.3 1.9 bitcast_convert_fusion.1
  90.9 2.1 bitcast_convert_fusion
  94.5 17.0 %shard_map.240 = (bf16[3,2,64,768]{3,2,1,0:T(8,128)(2,1)}, bf16[7,96,768]{2,1,0:T(8,128)(2,1)}) custom-call(bf16[2,256,768]{2,1,0:T(8,128)(2,1)} %convolution_convert_fusion.refs_0_, bf16[8,96,768]{2,1,0:T(8,128)(2,1)} %bitcast.149), custom_call_target="tpu_custom_call" | custom-call | tf_op jit(solution)/shard_map/pallas_call | solution.py:132
  111.5 1.9 convert_reduce_fusion.4
  113.4 2.1 convert_reduce_fusion.1
  121.3 2.1 fusion.18
  123.5 3.4 %multiply_reduce_fusion.2 = (f32[2,768]{1,0:T(2,128)}, bf16[2,64,768]{2,1,0:T(8,128)(2,1)}, f32[2,768]{1,0:T(2,128)}, f32[2,64]{1,0:T(2,128)S(1)}, f32[2,64]{1,0...) fusion(f32[2]{0:T(128)} %copy-done.60, bf16[2,256,768]{2,1,0:T(8,128)(2,1)} %param.27, s32[]{:T(128)S(6)} %select_n.52, ...), kind=kLoop, calls=%fused_computation.65 | loop fusion | flops 2649344 | bytes 2591756 | tf_op jit(solution)/shard_map/reduce_sum | solution.py:287
  126.9 1.9 multiply_reduce_fusion.9
  130.3 21.7 %shard_map.241 = (bf16[2,256,768]{2,1,0:T(8,128)(2,1)}, bf16[7,96,768]{2,1,0:T(8,128)(2,1)}) custom-call(bf16[2,64,768]{2,1,0:T(8,128)(2,1)} %multiply_convert_fusion.2.refs_0_, bf16[8,96,768]{2,1,0:T(8,128)(2,1)} %bitcast.147), custom_call_target="tpu_custom_call" | custom-call | tf_op jit(solution)/shard_map/pallas_call | solution.py:132
  152.0 2.3 convolution_convert_fusion.5
  154.3 3.1 %multiply_convert_fusion = bf16[2,3,256,256]{2,3,1,0:T(8,128)(2,1)} fusion(f32[2,3,256,256]{2,3,1,0:T(8,128)S(1)} %get-tuple-element.139, f32[2,3,256]{2,1,0:T(4,128)S(1)} %copy-done.31, bf16[2,256,3,64]{1,3,2,0:T(8,128)(2,1)} %bitcast.154, f32[2,256,3,64]{1,3,2,0:T(8,128)} %bitcast.146, f32[3,64]{1,0:T(4,128)S(1)} %copy-done.57), kind=kOutput, calls=%fused_computation.25 | convolution fusion | flops 103810816 | bytes 2956032 | tf_op jit(solution)/shard_map/sub | solution.py:299
  157.4 2.1 fusion.64
  159.5 3.3 %collective-permute-start.3 = (bf16[2,64,768]{2,1,0:T(8,128)(2,1)}, bf16[2,64,768]{2,1,0:T(8,128)(2,1)S(1)}, u32[]{:S(2)}, u32[]{:S(2)}) collective-permute-start(bf16[2,64,768]{2,1,0:T(8,128)(2,1)} %get-tuple-element.38), channel_id=1, source_target_pairs={{0,1},{1,2},{2,3},{3,0},{4,5},{5,6},{6,7},{7,4},{8,9},{9,10},{10,1... | collective-permute-start | bytes 589832 | tf_op jit(solution)/shard_map/ppermute | solution.py:148
  162.7 2.5 collective-permute-start.4
  168.5 1.9 fusion.32
  171.6 5.8 %collective-permute-done.4 = bf16[2,64,768]{2,1,0:T(8,128)(2,1)} collective-permute-done((bf16[2,64,768]{2,1,0:T(8,128)(2,1)}, bf16[2,64,768]{2,1,0:T(8,128)(2,1)}, u32[]{:S(2)}, u32[]{:S(2)}) %collective-permute-start.4) | collective-permute-done | bytes 196640 | tf_op jit(solution)/shard_map/ppermute | solution.py:148
  177.4 1.8 bitcast_convert_fusion.2
  180.7 3.2 %convolution_convert_fusion.2.refs_0_ = bf16[2,256,768]{2,1,0:T(8,128)(2,1)} fusion(bf16[2,256,576]{1,2,0:T(8,128)(2,1)S(1)} %pad_maximum_fusion, bf16[768,576,1]{0,1,2:T(8,128)(2,1)} %bitcast.163), kind=kOutput, calls=%fused_computation.40 | convolution fusion | flops 453378048 | bytes 2260992 | tf_op jit(solution)/shard_map/lsf,df->lsd/dot_general | solution.py:49
  184.7 19.8 %shard_map.242 = (bf16[3,2,64,768]{3,2,1,0:T(8,128)(2,1)}, bf16[7,96,576]{2,1,0:T(8,128)(2,1)}, bf16[7,96,192]{2,1,0:T(8,128)(2,1)}) custom-call(bf16[2,256,768]{2,1,0:T(8,128)(2,1)} %convolution_convert_fusion.2.refs_0_, bf16[8,96,576]{2,1,0:T(8,128)(2,1)} %bitcast.136, bf16[8,96,192]{2,1,0:T(8,128)(2,1)} %bitcast.139), custom_call_target="tpu_custom_call" | custom-call | tf_op jit(solution)/shard_map/pallas_call | solution.py:132
  208.0 20.0 %shard_map.243 = (bf16[2,256,768]{2,1,0:T(8,128)(2,1)}, f32[3,2,1152]{2,1,0:T(2,128)}, f32[4,1,768]{2,1,0:T(1,128)}) custom-call(bf16[2,64,768]{2,1,0:T(8,128)(2,1)} %add_convert_fusion.1.refs_0_, f32[4,2,1152]{2,1,0:T(2,128)} %bitcast.160, f32[1,768]{1,0:T(1,128)} %broadcast_in_dim.10.refs_2_), custom_call_target="tpu_custom_call" | custom-call | tf_op jit(solution)/shard_map/pallas_call | solution.py:132
  231.6 11.1 %shard_map.244 = (f32[8,1,4992]{2,1,0:T(1,128)}, f32[4,2,768]{2,1,0:T(2,128)}) custom-call(f32[1,4992]{1,0:T(1,128)} %broadcast_in_dim.11.refs_0_, f32[2,768]{1,0:T(2,128)} %fusion.54.refs_1_), custom_call_target="tpu_custom_call" | custom-call | tf_op jit(solution)/shard_map/pallas_call | solution.py:132
  251.2 1.8 fusion.42
  (242 shorter events, 56.2 us)
Async XLA Ops:
  0.7 14.3 %copy-start.1 = (bf16[2,256,768]{2,1,0:T(8,128)(2,1)S(1)}, bf16[2,256,768]{2,1,0:T(8,128)(2,1)}, u32[]{:S(2)}) copy-start(bf16[2,256,768]{2,1,0:T(8,128)(2,1)} %param.14) | copy-start | bytes 2359300
  2.1 13.4 %copy-start.67 = (bf16[768,3,192]{0,2,1:T(8,128)(2,1)S(1)}, bf16[768,3,192]{0,2,1:T(8,128)(2,1)}, u32[]{:S(2)}) copy-start(bf16[768,3,192]{0,2,1:T(8,128)(2,1)} %param.19) | copy-start | bytes 2654212
  76.3 47.2 %collective-permute-start = (bf16[2,64,768]{2,1,0:T(8,128)(2,1)}, bf16[2,64,768]{2,1,0:T(8,128)(2,1)}, u32[]{:S(2)}, u32[]{:S(2)}) collective-permute-start(bf16[2,64,768]{2,1,0:T(8,128)(2,1)} %get-tuple-element.117), channel_id=1, source_target_pairs={{0,1},{1,2},{2,3},{3,0},{4,5},{5,6},{6,7},{7,4},{8,9},{9,10},{10,1... | collective-permute-start | bytes 589832 | tf_op jit(solution)/shard_map/ppermute | solution.py:148
  80.0 43.4 %collective-permute-start.1 = (bf16[2,64,768]{2,1,0:T(8,128)(2,1)}, bf16[2,64,768]{2,1,0:T(8,128)(2,1)}, u32[]{:S(2)}, u32[]{:S(2)}) collective-permute-start(bf16[2,64,768]{2,1,0:T(8,128)(2,1)} %get-tuple-element.119), channel_id=1, source_target_pairs={{0,2},{1,3},{2,0},{3,1},{4,6},{5,7},{6,4},{7,5},{8,10},{9,11},{10,... | collective-permute-start | bytes 589832 | tf_op jit(solution)/shard_map/ppermute | solution.py:148
  82.2 41.3 %collective-permute-start.2 = (bf16[2,64,768]{2,1,0:T(8,128)(2,1)}, bf16[2,64,768]{2,1,0:T(8,128)(2,1)}, u32[]{:S(2)}, u32[]{:S(2)}) collective-permute-start(bf16[2,64,768]{2,1,0:T(8,128)(2,1)} %get-tuple-element.118), channel_id=1, source_target_pairs={{0,3},{1,0},{2,1},{3,2},{4,7},{5,4},{6,5},{7,6},{8,11},{9,8},{10,9... | collective-permute-start | bytes 589832 | tf_op jit(solution)/shard_map/ppermute | solution.py:148
  83.1 7.8 %copy-start.60 = (f32[2]{0:T(128)}, f32[2]{0:T(128)S(1)}, u32[]{:S(2)}) copy-start(f32[2]{0:T(128)S(1)} %compare_convert_fusion) | copy-start | bytes 28
  121.3 5.6 %copy-start.11 = (f32[2,64,768]{2,1,0:T(8,128)S(1)}, f32[2,64,768]{2,1,0:T(8,128)}, u32[]{:S(2)}) copy-start(f32[2,64,768]{2,1,0:T(8,128)} %convert_reduce_fusion.5) | copy-start | bytes 1179652
  121.3 5.6 %copy-start.37 = (f32[2,64]{1,0:T(2,128)S(1)}, f32[2,64]{1,0:T(2,128)}, u32[]{:S(2)}) copy-start(f32[2,64]{1,0:T(2,128)} %copy-done.36) | copy-start | bytes 1540
  121.3 5.6 %copy-start.48 = (f32[768]{0:T(1024)S(1)}, f32[768]{0:T(1024)}, u32[]{:S(2)}) copy-start(f32[768]{0:T(1024)} %param.22) | copy-start | bytes 9220
  121.3 5.6 %copy-start.50 = (f32[2,64]{1,0:T(2,128)S(1)}, f32[2,64]{1,0:T(2,128)}, u32[]{:S(2)}) copy-start(f32[2,64]{1,0:T(2,128)} %copy-done.49) | copy-start | bytes 1540
  121.3 5.6 %copy-start.61 = (f32[2]{0:T(128)S(1)}, f32[2]{0:T(128)}, u32[]{:S(2)}) copy-start(f32[2]{0:T(128)} %copy-done.60) | copy-start | bytes 28
  129.6 24.7 %copy-start.31 = (f32[2,3,256]{2,1,0:T(4,128)S(1)}, f32[2,3,256]{2,1,0:T(4,128)}, u32[]{:S(2)}) copy-start(f32[2,3,256]{2,1,0:T(4,128)} %log_add_fusion) | copy-start | bytes 18436
  130.3 24.0 %copy-start.57 = (f32[3,64]{1,0:T(4,128)S(1)}, f32[3,64]{1,0:T(4,128)}, u32[]{:S(2)}) copy-start(f32[3,64]{1,0:T(4,128)} %add.282) | copy-start | bytes 2308
  157.4 7.8 %copy-start.12 = (bf16[2,256,768]{2,1,0:T(8,128)(2,1)S(1)}, bf16[2,256,768]{2,1,0:T(8,128)(2,1)}, u32[]{:S(2)}) copy-start(bf16[2,256,768]{2,1,0:T(8,128)(2,1)} %get-tuple-element.39) | copy-start | bytes 2359300
  157.4 7.8 %copy-start.15 = (bf16[2,3,64,256]{3,2,1,0:T(8,128)(2,1)S(1)}, bf16[2,3,64,256]{3,2,1,0:T(8,128)(2,1)}, u32[]{:S(2)}) copy-start(bf16[2,3,64,256]{3,2,1,0:T(8,128)(2,1)} %copy-done.14) | copy-start | bytes 589828
  157.4 9.1 %copy-start.51 = (f32[768]{0:T(1024)S(1)}, f32[768]{0:T(1024)}, u32[]{:S(2)}) copy-start(f32[768]{0:T(1024)} %get-tuple-element.102) | copy-start | bytes 9220
  159.5 7.7 %copy-start.18 = (bf16[7,96,768]{2,1,0:T(8,128)(2,1)S(1)}, bf16[7,96,768]{2,1,0:T(8,128)(2,1)}, u32[]{:S(2)}) copy-start(bf16[7,96,768]{2,1,0:T(8,128)(2,1)} %get-tuple-element.56) | copy-start | bytes 3096580
  159.5 11.3 %collective-permute-start.3 = (bf16[2,64,768]{2,1,0:T(8,128)(2,1)}, bf16[2,64,768]{2,1,0:T(8,128)(2,1)S(1)}, u32[]{:S(2)}, u32[]{:S(2)}) collective-permute-start(bf16[2,64,768]{2,1,0:T(8,128)(2,1)} %get-tuple-element.38), channel_id=1, source_target_pairs={{0,1},{1,2},{2,3},{3,0},{4,5},{5,6},{6,7},{7,4},{8,9},{9,10},{10,1... | collective-permute-start | bytes 589832 | tf_op jit(solution)/shard_map/ppermute | solution.py:148
  162.7 14.7 %collective-permute-start.4 = (bf16[2,64,768]{2,1,0:T(8,128)(2,1)}, bf16[2,64,768]{2,1,0:T(8,128)(2,1)}, u32[]{:S(2)}, u32[]{:S(2)}) collective-permute-start(bf16[2,64,768]{2,1,0:T(8,128)(2,1)} %get-tuple-element.38), channel_id=1, source_target_pairs={{0,2},{1,3},{2,0},{3,1},{4,6},{5,7},{6,4},{7,5},{8,10},{9,11},{10,... | collective-permute-start | bytes 589832 | tf_op jit(solution)/shard_map/ppermute | solution.py:148
  165.2 18.7 %collective-permute-start.5 = (bf16[2,64,768]{2,1,0:T(8,128)(2,1)}, bf16[2,64,768]{2,1,0:T(8,128)(2,1)}, u32[]{:S(2)}, u32[]{:S(2)}) collective-permute-start(bf16[2,64,768]{2,1,0:T(8,128)(2,1)} %get-tuple-element.38), channel_id=1, source_target_pairs={{0,3},{1,0},{2,1},{3,2},{4,7},{5,4},{6,5},{7,6},{8,11},{9,8},{10,9... | collective-permute-start | bytes 589832 | tf_op jit(solution)/shard_map/ppermute | solution.py:148
  170.4 7.0 %copy-start.3 = (bf16[2,256,768]{2,1,0:T(8,128)(2,1)S(1)}, bf16[2,256,768]{2,1,0:T(8,128)(2,1)}, u32[]{:S(2)}) copy-start(bf16[2,256,768]{2,1,0:T(8,128)(2,1)} %param.14) | copy-start | bytes 2359300
  170.4 7.0 %copy-start.33 = (f32[2,768]{1,0:T(2,128)S(1)}, f32[2,768]{1,0:T(2,128)}, u32[]{:S(2)}) copy-start(f32[2,768]{1,0:T(2,128)} %copy-done.32) | copy-start | bytes 18436
  170.4 7.0 %copy-start.46 = (f32[2,256]{1,0:T(2,128)S(1)}, f32[2,256]{1,0:T(2,128)}, u32[]{:S(2)}) copy-start(f32[2,256]{1,0:T(2,128)} %copy-done.44) | copy-start | bytes 6148
  170.4 7.0 %copy-start.55 = (f32[2,256]{1,0:T(2,128)S(1)}, f32[2,256]{1,0:T(2,128)}, u32[]{:S(2)}) copy-start(f32[2,256]{1,0:T(2,128)} %copy-done.53) | copy-start | bytes 6148
  170.4 7.0 %copy-start.59 = (f32[2,768]{1,0:T(2,128)S(1)}, f32[2,768]{1,0:T(2,128)}, u32[]{:S(2)}) copy-start(f32[2,768]{1,0:T(2,128)} %copy-done.58) | copy-start | bytes 18436
  184.7 21.1 %copy-start.7 = (f32[2,256,768]{2,1,0:T(8,128)S(1)}, f32[2,256,768]{2,1,0:T(8,128)}, u32[]{:S(2)}) copy-start(f32[2,256,768]{2,1,0:T(8,128)} %subtract_multiply_fusion) | copy-start | bytes 4718596
  207.1 23.8 %copy-start.43 = (f32[4992]{0:T(1024)S(1)}, f32[4992]{0:T(1024)}, u32[]{:S(2)}) copy-start(f32[4992]{0:T(1024)} %custom-call) | copy-start | bytes 59908
  207.1 23.8 %copy-start.62 = (f32[768]{0:T(1024)S(1)}, f32[768]{0:T(1024)}, u32[]{:S(2)}) copy-start(f32[768]{0:T(1024)} %get-tuple-element.142) | copy-start | bytes 9220
  207.1 23.8 %copy-start.52 = (f32[768]{0:T(1024)S(1)}, f32[768]{0:T(1024)}, u32[]{:S(2)}) copy-start(f32[768]{0:T(1024)} %fusion.18) | copy-start | bytes 9220
  208.0 36.3 %copy-start.27 = (bf16[7,96,192]{2,1,0:T(8,128)(2,1)S(1)}, bf16[7,96,192]{2,1,0:T(8,128)(2,1)}, u32[]{:S(2)}) copy-start(bf16[7,96,192]{2,1,0:T(8,128)(2,1)} %get-tuple-element.54) | copy-start | bytes 774148
  229.5 16.4 %copy-start.20 = (bf16[7,96,576]{2,1,0:T(8,128)(2,1)S(1)}, bf16[7,96,576]{2,1,0:T(8,128)(2,1)}, u32[]{:S(2)}) copy-start(bf16[7,96,576]{2,1,0:T(8,128)(2,1)} %get-tuple-element.53) | copy-start | bytes 2322436
  247.3 5.7 %copy-start.23 = (bf16[2,256,768]{2,1,0:T(8,128)(2,1)S(1)}, bf16[2,256,768]{2,1,0:T(8,128)(2,1)}, u32[]{:S(2)}) copy-start(bf16[2,256,768]{2,1,0:T(8,128)(2,1)} %copy-done.22) | copy-start | bytes 2359300
  (44 other events, 98.8 us)
